TPU v7x, 256 devices: a whole 4x4x8 slice. The times are simulated.
256 devices in a mesh: brick: 32 (over y, z), grp: 8 (over x, core).
Axes of the slice: x: 4, y: 4, z: 8, core: 2. Of those that a mesh axis runs over, the one named last changes fastest.
Arguments:
- source: float32 [4, 256, 128, 512], P(None, 'brick', 'grp'), may hold values from -35 to 80
- phase_label: int32 [256, 128, 512], P('brick', 'grp'), may hold values from 0 to 2
- interface: int32 [256, 128, 512], P('brick', 'grp'), may hold values 0 or 1
- conductivity: float32 [2, 256, 128, 512], P(None, 'brick', 'grp'), may hold values from 0.3 to 3
- admittance: float32 [2, 256, 128, 512], P(None, 'brick', 'grp'), may hold values from 0.5 to 4
- extents: int32 [32, 8], P('brick'), may hold values from 1 to 128, 512 in all within a row
- coarse_inverse: float32 [1024, 1024], P('brick'), may hold values from -1 to 4
Outputs:
- solution: float32 [4, 256, 128, 512], P(None, 'brick', 'grp')
- residual: float32 [4, 256, 128, 512], P(None, 'brick', 'grp')
Inputs may be any that keep to these rules, and one draw needn't show every extreme that they name: `extents`: each brick's 8 slab lengths sum to 512; the longest is exactly 128.
All inputs are finite; a program needn't handle non-finite values. No bound on the sum of `interface` on one device may be relied on, other than what follows from the above.
Results may differ from a plain program's by a relative error of at most 0.0003.
Values sent between devices are 32-bit elements; how exact they have to be, the bound alone decides.
A program may use at most 64 MiB of HBM per device.

v0:
```python
import jax
import jax.numpy as jnp
from jax import lax
from jax.sharding import PartitionSpec as P

NZ = 512
KB = 8
ITERS = 3


EPS_SHIFT = 0.2
LOW_COND = 0.02
PRECISE = lax.Precision.HIGHEST


def padded_2(x, sides, width):
    for axis, dim in sides:
        count, length = (lax.axis_size(axis), x.shape[dim])
        up = [(i, (i + 1) % count) for i in range(count - 1)]
        down = [(j, i) for i, j in up]
        last = lax.slice_in_dim(x, length - width, length, axis=dim)
        first = lax.slice_in_dim(x, 0, width, axis=dim)
        before = lax.ppermute(last, axis, up)
        after = lax.ppermute(first, axis, down)
        x = jnp.concatenate([before, x, after], axis=dim)
    return x


def shifted(values, along, offset):
    count = values.shape[along]
    zero_shape = list(values.shape)
    zero_shape[along] = 1
    zeros = jnp.zeros(zero_shape, values.dtype)
    if offset > 0:
        return jnp.concatenate([lax.slice_in_dim(values, 1, count, axis=along), zeros], along)
    return jnp.concatenate([zeros, lax.slice_in_dim(values, 0, count - 1, axis=along)], along)


def neighbours(center, padded):
    return [
        padded[:, :-2, 1:-1],
        padded[:, 2:, 1:-1],
        padded[:, 1:-1, :-2],
        padded[:, 1:-1, 2:],
        shifted(center, 3, -1),
        shifted(center, 3, 1),
    ]


def apply_operator(fields, padded, weights, total_weight, charge_rate, storage_rate):
    gathered_sum = jnp.zeros_like(fields)
    for weight, values in zip(weights, neighbours(fields, padded)):
        gathered_sum = gathered_sum + jnp.repeat(weight, 2, axis=0) * values
    over_real = fields[0] - fields[2]
    over_imag = fields[1] - fields[3]
    flow_real = charge_rate * over_real - storage_rate * over_imag
    flow_imag = charge_rate * over_imag + storage_rate * over_real
    coupling = jnp.stack([flow_real, flow_imag, -flow_real, -flow_imag])
    return (jnp.repeat(total_weight, 2, axis=0) + EPS_SHIFT) * fields - gathered_sum + coupling


def local(source, phase_label, interface, conductivity, admittance, extents, coarse_inverse):
    conduct = jnp.stack(
        [
            conductivity[0] * jnp.where(phase_label == 1, 1.0, LOW_COND),
            conductivity[1] * jnp.where(phase_label == 2, 1.0, LOW_COND),
        ]
    )
    padded_cond = padded_2(conduct, (("brick", 1), ("grp", 2)), 1)
    weights = [0.5 * (conduct + values) for values in neighbours(conduct, padded_cond)]
    total_weight = jnp.zeros_like(conduct)
    for weight in weights:
        total_weight = total_weight + weight
    mask = interface.astype(jnp.float32)
    charge_rate = admittance[0] * mask
    storage_rate = admittance[1] * mask
    diagonal = jnp.repeat(total_weight, 2, axis=0) + EPS_SHIFT + charge_rate[None]
    slab_ends = jnp.cumsum(extents[0])
    starts = slab_ends - extents[0]
    depth = jnp.arange(NZ)
    onehot = ((depth[:, None] >= starts[None, :]) & (depth[:, None] < slab_ends[None, :])).astype(
        jnp.float32
    )
    width = 4 * KB
    slab_cells = float(source.shape[1] * source.shape[2] * lax.axis_size("grp") * (NZ // KB))
    solution = jnp.zeros_like(source)
    residual = source
    for iteration in range(ITERS):
        plane = residual.sum(axis=(1, 2))
        part_sum = (jnp.dot(plane, onehot, precision=PRECISE) / slab_cells).reshape(1, width)
        group_sum = lax.psum(part_sum, "grp")
        full_coarse = lax.all_gather(group_sum, "brick", axis=0, tiled=True)
        first = residual / diagonal
        local_image = apply_operator(
            first,
            jnp.pad(first, ((0, 0), (1, 1), (1, 1), (0, 0))),
            weights,
            total_weight,
            charge_rate,
            storage_rate,
        )
        second = first + (residual - local_image) / diagonal
        correction = jnp.dot(coarse_inverse, full_coarse.reshape(-1), precision=PRECISE).reshape(
            4, KB
        )
        profile = jnp.dot(correction, onehot.T, precision=PRECISE)
        search = second + profile[:, None, None, :]
        image = apply_operator(
            search,
            padded_2(search, (("brick", 1), ("grp", 2)), 1),
            weights,
            total_weight,
            charge_rate,
            storage_rate,
        )
        product_ri, product_ii = lax.psum(
            (jnp.sum(residual * image), jnp.sum(image * image)), ("brick", "grp")
        )
        alpha = product_ri / (product_ii + 1e-06)
        solution = solution + alpha * search
        residual = residual - alpha * image
    return (solution, residual)


def solution(mesh):
    placed = (
        P(None, "brick", "grp", None),
        P("brick", "grp", None),
        P("brick", "grp", None),
        P(None, "brick", "grp", None),
        P(None, "brick", "grp", None),
        P("brick", None),
        P("brick", None),
    )
    return jax.shard_map(
        local,
        mesh=mesh,
        in_specs=placed,
        out_specs=(P(None, "brick", "grp", None), P(None, "brick", "grp", None)),
        check_vma=False,
    )
```

profile of v0, /device:TPU:1, one launch (start us, length us, event | category | flops | bytes accessed | tf_op | source)
XLA Modules:
  0.0 515.7 jit_solution(12663626029740458696)
XLA Ops:
  0.7 1.3 fusion.79
  2.0 4.4 collective-permute-start
  6.4 1.3 collective-permute-start.1
  7.9 3.6 collective-permute-done.1
  11.6 3.8 collective-permute-start.3
  15.5 3.0 collective-permute-start.2
  18.7 0.8 collective-permute-done.2
  19.6 3.1 add_add_fusion
  22.9 0.9 copy-done.35
  24.2 1.0 negate_bitcast_fusion.11
  25.1 1.7 fusion.118
  27.2 12.9 %psum.63 = f32[1,32]{1,0:T(1,128)S(1)} all-reduce(f32[1,32]{1,0:T(1,128)S(1)} %reshape.119), channel_id=1, replica_groups=mesh['brick'=32,'grp'=8] {'grp'}, use_global_device_ids=true, to_apply=%region_2.3 | all-reduce | flops 32 | bytes 256 | tf_op jit(solution)/shard_map/psum | solution.py:91
  40.1 33.3 %all-gather = f32[32,1,32]{2,1,0:T(1,128)S(1)} all-gather(f32[1,1,32]{2,1,0:T(1,128)S(1)} %bitcast.460), channel_id=1, replica_groups=mesh['brick'=32,'grp'=8] {'brick'}, dimensions={0}, use_global_device_ids=true | all-gather | bytes 4224 | tf_op jit(solution)/shard_map/all_gather | solution.py:92
  73.4 0.6 broadcast.78
  73.9 0.7 reduce.9
  74.7 1.0 fusion.86
  76.1 0.8 copy-done.11
  77.5 3.1 fusion.7
  80.6 2.8 collective-permute-start.4
  83.4 1.3 collective-permute-start.5
  84.7 0.4 fusion.116
  85.3 3.8 collective-permute-done.5
  89.2 12.1 %collective-permute-start.6 = (f32[4,10,1,512]{3,2,1,0:T(1,128)S(1)}, f32[4,10,1,512]{3,2,1,0:T(1,128)S(1)}, u32[]{:S(2)}, u32[]{:S(2)}) collective-permute-start(f32[4,10,1,512]{3,2,1,0:T(1,128)S(1)} %get-tuple-element.67), channel_id=1, source_target_pairs={{0,1},{1,2},{2,3},{3,4},{4,5},{5,6},{6,7},{8,9},{9,10},{10,11},{11... | collective-permute-start | bytes 245768 | tf_op jit(solution)/shard_map/ppermute | solution.py:23
  101.3 3.3 collective-permute-start.7
  104.8 2.4 collective-permute-done.7
  107.2 3.2 multiply_reduce_fusion.4
  110.5 76.9 %all-reduce.19 = (f32[]{:T(128)}, f32[]{:T(128)}) all-reduce(f32[]{:T(128)} %get-tuple-element.7, f32[]{:T(128)} %get-tuple-element.6), channel_id=1, replica_groups=mesh['brick'=32,'grp'=8] {'brick','grp'}, use_global_device_ids=true, to_apply=%region_4.5 | all-reduce | flops 2 | bytes 16 | tf_op jit(solution)/shard_map/psum | solution.py:116
  188.6 1.5 fusion.103
  190.3 0.8 copy-done.7
  191.3 1.3 negate_bitcast_fusion.7
  192.6 1.7 fusion.114
  194.6 12.4 %psum.66 = f32[1,32]{1,0:T(1,128)S(1)} all-reduce(f32[1,32]{1,0:T(1,128)S(1)} %reshape.121), channel_id=1, replica_groups=mesh['brick'=32,'grp'=8] {'grp'}, use_global_device_ids=true, to_apply=%region_8.9 | all-reduce | flops 32 | bytes 256 | tf_op jit(solution)/shard_map/psum | solution.py:91
  207.1 27.6 %all-gather.1 = f32[32,1,32]{2,1,0:T(1,128)S(1)} all-gather(f32[1,1,32]{2,1,0:T(1,128)S(1)} %bitcast.461), channel_id=1, replica_groups=mesh['brick'=32,'grp'=8] {'brick'}, dimensions={0}, use_global_device_ids=true | all-gather | bytes 4224 | tf_op jit(solution)/shard_map/all_gather | solution.py:92
  234.7 0.7 reduce.10
  235.5 1.0 fusion.84
  236.7 6.8 %fusion.9 = f32[4,8,16,512]{3,2,1,0:T(8,128)S(1)} fusion(f32[4,8,16,512]{3,2,1,0:T(8,128)} %copy-done.4, f32[4,8,16,512]{3,2,1,0:T(8,128)} %copy-done.7, f32[1,8,16,512]{3,2,1,0:T(8,128)} %get-tuple-element.59, f32[1,8,16,512]{3,2,1,0:T(8,128)} %get-tuple-element.32, f32[1,8,16,512]{3,2,1,0:T(8,128)} %bitcast.451, f32[1,8,16,512]{3,2,1,0:T(8,128)} %bitcast.450, ...), kind=kLoop, calls=%fused_computation.67 | loop fusion | flops 5767168 | bytes 10227712 | tf_op jit(solution)/shard_map/add | solution.py:107
  243.5 2.0 collective-permute-start.8
  245.5 1.3 collective-permute-start.9
  246.8 0.4 fusion.113
  247.4 3.8 collective-permute-done.9
  251.4 11.5 %collective-permute-start.10 = (f32[4,10,1,512]{3,2,1,0:T(1,128)S(1)}, f32[4,10,1,512]{3,2,1,0:T(1,128)S(1)}, u32[]{:S(2)}, u32[]{:S(2)}) collective-permute-start(f32[4,10,1,512]{3,2,1,0:T(1,128)S(1)} %get-tuple-element.65), channel_id=1, source_target_pairs={{0,1},{1,2},{2,3},{3,4},{4,5},{5,6},{6,7},{8,9},{9,10},{10,11},{11... | collective-permute-start | bytes 245768 | tf_op jit(solution)/shard_map/ppermute | solution.py:23
  262.9 3.4 collective-permute-start.11
  266.6 2.2 collective-permute-done.11
  268.9 3.3 multiply_reduce_fusion.2
  272.1 76.6 %all-reduce.18 = (f32[]{:T(128)}, f32[]{:T(128)}) all-reduce(f32[]{:T(128)} %get-tuple-element.5, f32[]{:T(128)} %get-tuple-element.4), channel_id=1, replica_groups=mesh['brick'=32,'grp'=8] {'brick','grp'}, use_global_device_ids=true, to_apply=%region_10.11 | all-reduce | flops 2 | bytes 16 | tf_op jit(solution)/shard_map/psum | solution.py:116
  350.0 1.8 fusion.101
  352.1 0.7 copy-done.5
  353.0 1.3 negate_bitcast_fusion.3
  354.3 1.7 fusion.111
  356.4 12.7 %psum.69 = f32[1,32]{1,0:T(1,128)S(1)} all-reduce(f32[1,32]{1,0:T(1,128)S(1)} %reshape.123), channel_id=1, replica_groups=mesh['brick'=32,'grp'=8] {'grp'}, use_global_device_ids=true, to_apply=%region_14.15 | all-reduce | flops 32 | bytes 256 | tf_op jit(solution)/shard_map/psum | solution.py:91
  369.0 26.8 %all-gather.2 = f32[32,1,32]{2,1,0:T(1,128)S(1)} all-gather(f32[1,1,32]{2,1,0:T(1,128)S(1)} %bitcast.462), channel_id=1, replica_groups=mesh['brick'=32,'grp'=8] {'brick'}, dimensions={0}, use_global_device_ids=true | all-gather | bytes 4224 | tf_op jit(solution)/shard_map/all_gather | solution.py:92
  395.9 0.7 reduce.11
  396.6 1.0 fusion.82
  397.8 7.0 %fusion.11 = f32[4,8,16,512]{3,2,1,0:T(8,128)S(1)} fusion(f32[4,8,16,512]{3,2,1,0:T(8,128)} %copy-done.3, f32[4,8,16,512]{3,2,1,0:T(8,128)} %copy-done.5, f32[1,8,16,512]{3,2,1,0:T(8,128)} %get-tuple-element.55, f32[1,8,16,512]{3,2,1,0:T(8,128)} %get-tuple-element.21, f32[1,8,16,512]{3,2,1,0:T(8,128)} %bitcast.449, f32[1,8,16,512]{3,2,1,0:T(8,128)} %bitcast.448, ...), kind=kLoop, calls=%fused_computation.69 | loop fusion | flops 5767168 | bytes 10227712 | tf_op jit(solution)/shard_map/add | solution.py:107
  404.9 2.7 collective-permute-start.12
  407.6 1.3 collective-permute-start.13
  408.9 0.4 fusion.110
  409.5 3.8 collective-permute-done.13
  413.4 11.9 %collective-permute-start.14 = (f32[4,10,1,512]{3,2,1,0:T(1,128)S(1)}, f32[4,10,1,512]{3,2,1,0:T(1,128)S(1)}, u32[]{:S(2)}, u32[]{:S(2)}) collective-permute-start(f32[4,10,1,512]{3,2,1,0:T(1,128)S(1)} %get-tuple-element.63), channel_id=1, source_target_pairs={{0,1},{1,2},{2,3},{3,4},{4,5},{5,6},{6,7},{8,9},{9,10},{10,11},{11... | collective-permute-start | bytes 245768 | tf_op jit(solution)/shard_map/ppermute | solution.py:23
  425.4 3.3 collective-permute-start.15
  428.9 2.4 collective-permute-done.15
  431.3 3.3 multiply_reduce_fusion
  434.6 76.3 %all-reduce.17 = (f32[]{:T(128)}, f32[]{:T(128)}) all-reduce(f32[]{:T(128)} %get-tuple-element.3, f32[]{:T(128)} %get-tuple-element.2), channel_id=1, replica_groups=mesh['brick'=32,'grp'=8] {'brick','grp'}, use_global_device_ids=true, to_apply=%region_16.17 | all-reduce | flops 2 | bytes 16 | tf_op jit(solution)/shard_map/psum | solution.py:116
  512.2 3.5 multiply_subtract_fusion
  (119 shorter events, 6.4 us)
Async XLA Ops:
  0.6 74.1 %copy-start = (f32[32,1024]{1,0:T(8,128)S(1)}, f32[32,1024]{1,0:T(8,128)}, u32[]{:S(2)}) copy-start(f32[32,1024]{1,0:T(8,128)} %param.13) | copy-start | bytes 393220
  0.6 7.0 %copy-start.41 = (s32[1,8]{1,0:T(1,128)S(1)}, s32[1,8]{1,0:T(1,128)}, u32[]{:S(2)}) copy-start(s32[1,8]{1,0:T(1,128)} %param.12) | copy-start | bytes 100
  0.7 7.2 %copy-start.37 = (f32[2,8,16,512]{3,2,1,0:T(8,128)S(1)}, f32[2,8,16,512]{3,2,1,0:T(8,128)}, u32[]{:S(2)}) copy-start(f32[2,8,16,512]{3,2,1,0:T(8,128)} %param.11) | copy-start | bytes 1572868
  0.7 7.2 %copy-start.34 = (s32[8,16,512]{2,1,0:T(8,128)S(1)}, s32[8,16,512]{2,1,0:T(8,128)}, u32[]{:S(2)}) copy-start(s32[8,16,512]{2,1,0:T(8,128)} %param.9) | copy-start | bytes 786436
  2.0 5.9 %collective-permute-start = (f32[2,1,16,512]{3,2,1,0:T(8,128)S(1)}, f32[2,1,16,512]{3,2,1,0:T(8,128)S(1)}, u32[]{:S(2)}, u32[]{:S(2)}) collective-permute-start(f32[2,1,16,512]{3,2,1,0:T(8,128)S(1)} %get-tuple-element.95), channel_id=1, source_target_pairs={{0,8},{8,16},{16,24},{24,32},{32,40},{40,48},{48,56},{56,64},{64,7... | collective-permute-start | bytes 196616 | tf_op jit(solution)/shard_map/ppermute | solution.py:23
  6.4 5.2 %collective-permute-start.1 = (f32[2,1,16,512]{3,2,1,0:T(8,128)S(1)}, f32[2,1,16,512]{3,2,1,0:T(8,128)S(1)}, u32[]{:S(2)}, u32[]{:S(2)}) collective-permute-start(f32[2,1,16,512]{3,2,1,0:T(8,128)S(1)} %get-tuple-element.96), channel_id=1, source_target_pairs={{8,0},{16,8},{24,16},{32,24},{40,32},{48,40},{56,48},{64,56},{72,6... | collective-permute-start | bytes 196616 | tf_op jit(solution)/shard_map/ppermute | solution.py:24
  7.9 10.8 %copy-start.39 = (f32[2,1,16,512]{3,2,1,0:T(8,128)}, f32[2,1,16,512]{3,2,1,0:T(8,128)S(1)}, u32[]{:S(2)}) copy-start(f32[2,1,16,512]{3,2,1,0:T(8,128)S(1)} %collective-permute-done) | copy-start | bytes 196612
  11.6 7.2 %copy-start.40 = (f32[2,1,16,512]{3,2,1,0:T(8,128)}, f32[2,1,16,512]{3,2,1,0:T(8,128)S(1)}, u32[]{:S(2)}) copy-start(f32[2,1,16,512]{3,2,1,0:T(8,128)S(1)} %collective-permute-done.1) | copy-start | bytes 196612
  11.6 7.1 %collective-permute-start.3 = (f32[2,10,1,512]{3,2,1,0:T(1,128)S(1)}, f32[2,10,1,512]{3,2,1,0:T(1,128)S(1)}, u32[]{:S(2)}, u32[]{:S(2)}) collective-permute-start(f32[2,10,1,512]{3,2,1,0:T(1,128)S(1)} %get-tuple-element.91), channel_id=1, source_target_pairs={{1,0},{2,1},{3,2},{4,3},{5,4},{6,5},{7,6},{9,8},{10,9},{11,10},{12... | collective-permute-start | bytes 122888 | tf_op jit(solution)/shard_map/ppermute | solution.py:24
  15.5 4.1 collective-permute-start.2
  19.6 3.1 copy-start.26
  22.6 246.2 %copy-start.9 = (f32[2,8,16,512]{3,2,1,0:T(8,128)}, f32[2,8,16,512]{3,2,1,0:T(8,128)S(1)}, u32[]{:S(2)}) copy-start(f32[2,8,16,512]{3,2,1,0:T(8,128)S(1)} %get-tuple-element.47) | copy-start | bytes 1572868
  22.6 329.2 %copy-start.1 = (f32[2,8,16,512]{3,2,1,0:T(8,128)}, f32[2,8,16,512]{3,2,1,0:T(8,128)S(1)}, u32[]{:S(2)}) copy-start(f32[2,8,16,512]{3,2,1,0:T(8,128)S(1)} %get-tuple-element.46) | copy-start | bytes 1572868
  22.7 1.2 copy-start.35
  22.7 1.5 copy-start.38
  25.1 50.8 %copy-start.28 = (f32[8,16,512]{2,1,0:T(8,128)}, f32[8,16,512]{2,1,0:T(8,128)S(1)}, u32[]{:S(2)}) copy-start(f32[8,16,512]{2,1,0:T(8,128)S(1)} %get-tuple-element.43) | copy-start | bytes 786436
  74.7 1.4 copy-start.36
  75.9 1.1 copy-start.11
  75.9 1.2 copy-start.14
  75.9 1.4 copy-start.17
  76.0 1.5 copy-start.20
  80.6 4.7 collective-permute-start.4
  83.4 5.7 %collective-permute-start.5 = (f32[4,1,16,512]{3,2,1,0:T(8,128)S(1)}, f32[4,1,16,512]{3,2,1,0:T(8,128)S(1)}, u32[]{:S(2)}, u32[]{:S(2)}) collective-permute-start(f32[4,1,16,512]{3,2,1,0:T(8,128)S(1)} %get-tuple-element.82), channel_id=1, source_target_pairs={{8,0},{16,8},{24,16},{32,24},{40,32},{48,40},{56,48},{64,56},{72,6... | collective-permute-start | bytes 393224 | tf_op jit(solution)/shard_map/ppermute | solution.py:24
  85.0 19.6 %copy-start.29 = (f32[8,16,512]{2,1,0:T(8,128)S(1)}, f32[8,16,512]{2,1,0:T(8,128)}, u32[]{:S(2)}) copy-start(f32[8,16,512]{2,1,0:T(8,128)} %copy-done.28) | copy-start | bytes 786436
  89.2 15.6 %collective-permute-start.6 = (f32[4,10,1,512]{3,2,1,0:T(1,128)S(1)}, f32[4,10,1,512]{3,2,1,0:T(1,128)S(1)}, u32[]{:S(2)}, u32[]{:S(2)}) collective-permute-start(f32[4,10,1,512]{3,2,1,0:T(1,128)S(1)} %get-tuple-element.67), channel_id=1, source_target_pairs={{0,1},{1,2},{2,3},{3,4},{4,5},{5,6},{6,7},{8,9},{9,10},{10,11},{11... | collective-permute-start | bytes 245768 | tf_op jit(solution)/shard_map/ppermute | solution.py:23
  101.3 5.9 %copy-start.23 = (f32[2,8,16,512]{3,2,1,0:T(8,128)S(1)}, f32[2,8,16,512]{3,2,1,0:T(8,128)}, u32[]{:S(2)}) copy-start(f32[2,8,16,512]{3,2,1,0:T(8,128)} %get-tuple-element.52) | copy-start | bytes 1572868
  101.3 5.9 %copy-start.27 = (f32[4,8,16,512]{3,2,1,0:T(8,128)S(1)}, f32[4,8,16,512]{3,2,1,0:T(8,128)}, u32[]{:S(2)}) copy-start(f32[4,8,16,512]{3,2,1,0:T(8,128)} %param.7) | copy-start | bytes 3145732
  101.3 5.9 %collective-permute-start.7 = (f32[4,10,1,512]{3,2,1,0:T(1,128)S(1)}, f32[4,10,1,512]{3,2,1,0:T(1,128)S(1)}, u32[]{:S(2)}, u32[]{:S(2)}) collective-permute-start(f32[4,10,1,512]{3,2,1,0:T(1,128)S(1)} %get-tuple-element.68), channel_id=1, source_target_pairs={{1,0},{2,1},{3,2},{4,3},{5,4},{6,5},{7,6},{9,8},{10,9},{11,10},{12... | collective-permute-start | bytes 245768 | tf_op jit(solution)/shard_map/ppermute | solution.py:24
  190.1 1.0 copy-start.7
  190.1 1.1 copy-start.30
  191.3 3.0 copy-start.4
  243.5 4.0 collective-permute-start.8
  245.5 5.7 %collective-permute-start.9 = (f32[4,1,16,512]{3,2,1,0:T(8,128)S(1)}, f32[4,1,16,512]{3,2,1,0:T(8,128)S(1)}, u32[]{:S(2)}, u32[]{:S(2)}) collective-permute-start(f32[4,1,16,512]{3,2,1,0:T(8,128)S(1)} %get-tuple-element.76), channel_id=1, source_target_pairs={{8,0},{16,8},{24,16},{32,24},{40,32},{48,40},{56,48},{64,56},{72,6... | collective-permute-start | bytes 393224 | tf_op jit(solution)/shard_map/ppermute | solution.py:24
  247.2 19.2 %copy-start.31 = (f32[8,16,512]{2,1,0:T(8,128)S(1)}, f32[8,16,512]{2,1,0:T(8,128)}, u32[]{:S(2)}) copy-start(f32[8,16,512]{2,1,0:T(8,128)} %copy-done.28) | copy-start | bytes 786436
  251.2 17.6 %copy-start.21 = (f32[2,8,16,512]{3,2,1,0:T(8,128)S(1)}, f32[2,8,16,512]{3,2,1,0:T(8,128)}, u32[]{:S(2)}) copy-start(f32[2,8,16,512]{3,2,1,0:T(8,128)} %get-tuple-element.51) | copy-start | bytes 1572868
  251.2 17.6 %copy-start.24 = (f32[2,8,16,512]{3,2,1,0:T(8,128)S(1)}, f32[2,8,16,512]{3,2,1,0:T(8,128)}, u32[]{:S(2)}) copy-start(f32[2,8,16,512]{3,2,1,0:T(8,128)} %get-tuple-element.52) | copy-start | bytes 1572868
  251.4 15.2 %collective-permute-start.10 = (f32[4,10,1,512]{3,2,1,0:T(1,128)S(1)}, f32[4,10,1,512]{3,2,1,0:T(1,128)S(1)}, u32[]{:S(2)}, u32[]{:S(2)}) collective-permute-start(f32[4,10,1,512]{3,2,1,0:T(1,128)S(1)} %get-tuple-element.65), channel_id=1, source_target_pairs={{0,1},{1,2},{2,3},{3,4},{4,5},{5,6},{6,7},{8,9},{9,10},{10,11},{11... | collective-permute-start | bytes 245768 | tf_op jit(solution)/shard_map/ppermute | solution.py:23
  262.9 5.9 %copy-start.8 = (f32[4,8,16,512]{3,2,1,0:T(8,128)S(1)}, f32[4,8,16,512]{3,2,1,0:T(8,128)}, u32[]{:S(2)}) copy-start(f32[4,8,16,512]{3,2,1,0:T(8,128)} %copy-done.7) | copy-start | bytes 3145732
  262.9 5.9 %copy-start.12 = (f32[2,8,16,512]{3,2,1,0:T(8,128)S(1)}, f32[2,8,16,512]{3,2,1,0:T(8,128)}, u32[]{:S(2)}) copy-start(f32[2,8,16,512]{3,2,1,0:T(8,128)} %get-tuple-element.48) | copy-start | bytes 1572868
  262.9 5.9 %copy-start.15 = (f32[2,8,16,512]{3,2,1,0:T(8,128)S(1)}, f32[2,8,16,512]{3,2,1,0:T(8,128)}, u32[]{:S(2)}) copy-start(f32[2,8,16,512]{3,2,1,0:T(8,128)} %get-tuple-element.49) | copy-start | bytes 1572868
  262.9 5.9 %copy-start.18 = (f32[2,8,16,512]{3,2,1,0:T(8,128)S(1)}, f32[2,8,16,512]{3,2,1,0:T(8,128)}, u32[]{:S(2)}) copy-start(f32[2,8,16,512]{3,2,1,0:T(8,128)} %get-tuple-element.50) | copy-start | bytes 1572868
  262.9 5.9 %collective-permute-start.11 = (f32[4,10,1,512]{3,2,1,0:T(1,128)S(1)}, f32[4,10,1,512]{3,2,1,0:T(1,128)S(1)}, u32[]{:S(2)}, u32[]{:S(2)}) collective-permute-start(f32[4,10,1,512]{3,2,1,0:T(1,128)S(1)} %get-tuple-element.66), channel_id=1, source_target_pairs={{1,0},{2,1},{3,2},{4,3},{5,4},{6,5},{7,6},{9,8},{10,9},{11,10},{12... | collective-permute-start | bytes 245768 | tf_op jit(solution)/shard_map/ppermute | solution.py:24
  351.8 1.0 copy-start.5
  351.9 1.2 copy-start.32
  353.0 3.0 copy-start.3
  404.9 4.6 collective-permute-start.12
  407.6 5.7 %collective-permute-start.13 = (f32[4,1,16,512]{3,2,1,0:T(8,128)S(1)}, f32[4,1,16,512]{3,2,1,0:T(8,128)S(1)}, u32[]{:S(2)}, u32[]{:S(2)}) collective-permute-start(f32[4,1,16,512]{3,2,1,0:T(8,128)S(1)} %get-tuple-element.70), channel_id=1, source_target_pairs={{8,0},{16,8},{24,16},{32,24},{40,32},{48,40},{56,48},{64,56},{72,6... | collective-permute-start | bytes 393224 | tf_op jit(solution)/shard_map/ppermute | solution.py:24
  408.9 22.4 %copy-start.22 = (f32[2,8,16,512]{3,2,1,0:T(8,128)S(1)}, f32[2,8,16,512]{3,2,1,0:T(8,128)}, u32[]{:S(2)}) copy-start(f32[2,8,16,512]{3,2,1,0:T(8,128)} %get-tuple-element.51) | copy-start | bytes 1572868
  408.9 22.4 %copy-start.25 = (f32[2,8,16,512]{3,2,1,0:T(8,128)S(1)}, f32[2,8,16,512]{3,2,1,0:T(8,128)}, u32[]{:S(2)}) copy-start(f32[2,8,16,512]{3,2,1,0:T(8,128)} %get-tuple-element.52) | copy-start | bytes 1572868
  409.3 19.4 %copy-start.33 = (f32[8,16,512]{2,1,0:T(8,128)S(1)}, f32[8,16,512]{2,1,0:T(8,128)}, u32[]{:S(2)}) copy-start(f32[8,16,512]{2,1,0:T(8,128)} %copy-done.28) | copy-start | bytes 786436
  413.3 18.0 %copy-start.16 = (f32[2,8,16,512]{3,2,1,0:T(8,128)S(1)}, f32[2,8,16,512]{3,2,1,0:T(8,128)}, u32[]{:S(2)}) copy-start(f32[2,8,16,512]{3,2,1,0:T(8,128)} %get-tuple-element.49) | copy-start | bytes 1572868
  413.3 18.0 %copy-start.19 = (f32[2,8,16,512]{3,2,1,0:T(8,128)S(1)}, f32[2,8,16,512]{3,2,1,0:T(8,128)}, u32[]{:S(2)}) copy-start(f32[2,8,16,512]{3,2,1,0:T(8,128)} %get-tuple-element.50) | copy-start | bytes 1572868
  413.4 15.4 %collective-permute-start.14 = (f32[4,10,1,512]{3,2,1,0:T(1,128)S(1)}, f32[4,10,1,512]{3,2,1,0:T(1,128)S(1)}, u32[]{:S(2)}, u32[]{:S(2)}) collective-permute-start(f32[4,10,1,512]{3,2,1,0:T(1,128)S(1)} %get-tuple-element.63), channel_id=1, source_target_pairs={{0,1},{1,2},{2,3},{3,4},{4,5},{5,6},{6,7},{8,9},{9,10},{10,11},{11... | collective-permute-start | bytes 245768 | tf_op jit(solution)/shard_map/ppermute | solution.py:23
  425.3 6.0 %copy-start.2 = (f32[2,8,16,512]{3,2,1,0:T(8,128)S(1)}, f32[2,8,16,512]{3,2,1,0:T(8,128)}, u32[]{:S(2)}) copy-start(f32[2,8,16,512]{3,2,1,0:T(8,128)} %copy-done.1) | copy-start | bytes 1572868
  425.3 6.0 %copy-start.6 = (f32[4,8,16,512]{3,2,1,0:T(8,128)S(1)}, f32[4,8,16,512]{3,2,1,0:T(8,128)}, u32[]{:S(2)}) copy-start(f32[4,8,16,512]{3,2,1,0:T(8,128)} %copy-done.5) | copy-start | bytes 3145732
  425.3 6.0 %copy-start.10 = (f32[2,8,16,512]{3,2,1,0:T(8,128)S(1)}, f32[2,8,16,512]{3,2,1,0:T(8,128)}, u32[]{:S(2)}) copy-start(f32[2,8,16,512]{3,2,1,0:T(8,128)} %copy-done.9) | copy-start | bytes 1572868
  425.4 6.0 %copy-start.13 = (f32[2,8,16,512]{3,2,1,0:T(8,128)S(1)}, f32[2,8,16,512]{3,2,1,0:T(8,128)}, u32[]{:S(2)}) copy-start(f32[2,8,16,512]{3,2,1,0:T(8,128)} %get-tuple-element.48) | copy-start | bytes 1572868
  425.4 5.9 %collective-permute-start.15 = (f32[4,10,1,512]{3,2,1,0:T(1,128)S(1)}, f32[4,10,1,512]{3,2,1,0:T(1,128)S(1)}, u32[]{:S(2)}, u32[]{:S(2)}) collective-permute-start(f32[4,10,1,512]{3,2,1,0:T(1,128)S(1)} %get-tuple-element.64), channel_id=1, source_target_pairs={{1,0},{2,1},{3,2},{4,3},{5,4},{6,5},{7,6},{9,8},{10,9},{11,10},{12... | collective-permute-start | bytes 245768 | tf_op jit(solution)/shard_map/ppermute | solution.py:24
where the time goes:
time: 517 us; the launch traced here: 516 us
  blocking collectives  356 us (69%)
  starting transfers between devices  69.4 us (13%)
  other arithmetic  45.7 us (9%)
  waiting for transfers between devices  23.5 us (5%)
  local copies, waits for them, and re-layouts  12 us (2%)
  between operations  5.19 us (1%)
    psum x3, blocking collectives, local(): lax.psum((jnp.sum(residual * image), jnp.sum(image * image)), ('brick', '...  230 us
    all_gather x3, blocking collectives, local(): full_coarse = lax.all_gather(group_sum, 'brick', axis=0, tiled=True)  87.7 us
    ppermute x8, starting transfers between devices, padded_2(): before = lax.ppermute(last, axis, up)  50.4 us
    psum x3, blocking collectives, local(): group_sum = lax.psum(part_sum, 'grp')  38 us
    ppermute x8, waiting for transfers between devices, padded_2(): after = lax.ppermute(first, axis, down)  22 us
    ppermute x8, starting transfers between devices, padded_2(): after = lax.ppermute(first, axis, down)  19 us
    add x3, other arithmetic, local(): search = second + profile[:, None, None, :]  16.9 us
  transfers between devices with their start and end apart: 16, of which 11 were waited for; matrix products, arithmetic and copies ran while one was open for 0% of the time, Pallas kernels for 0%

commit v1 on v0

v1 whole, which is shorter than its diff:
```python
import jax
import jax.numpy as jnp
from jax import lax
from jax.experimental import pallas as pl
from jax.experimental.pallas import tpu as pltpu
from jax.sharding import PartitionSpec as P

CX, CY, NZ, KB = 8, 16, 512, 8
ITERS = 3
SLAB_CELLS = 65536.0
EPS_SHIFT = 0.2
LOW_COND = 0.02
LANES = 128
TILES = NZ // LANES
MESH = pl.DeviceIdType.MESH
F32 = jnp.float32


def roll(v, shift, axis):
    return pltpu.roll(v, shift % v.shape[axis], axis)


def kernel(
    ext, src_h, phase_h, inter_h, cond_h, adm_h, cinv_h, sol_h, res_h,
    r, q, u, z, sol, first, second, cond, phase, inter, adm, cd, cr, sr,
    wx, wym, wyp, wzm, wzp, tw, ee, dinv, wyb, cinv, onehot, table,
    hxc, hyc, syc, hx, hy, sy, row_g, slots_g, slots_y, slots_z, row_c, slots_c, row_all, slots_all, sizes,
    load_sem, out_sem, near_send, near_recv, c_sem, halo_sem, p0_send, p0_recv, core_sem, all_send, all_recv,
):
    brick, grp = lax.axis_index("brick"), lax.axis_index("grp")
    cy, cz, cx, core = brick // 8, brick % 8, grp // 2, grp % 2
    up = {"brick": (brick + 1) % 32, "grp": grp}
    down = {"brick": (brick + 31) % 32, "grp": grp}
    right = {"brick": brick, "grp": (grp + 1) % 8}
    left = {"brick": brick, "grp": (grp + 7) % 8}
    group = [{"brick": brick, "grp": (grp + j) % 8} for j in (4, 5, 3, 2, 6, 1, 7)]
    along_y = [{"brick": ((cy + j) % 4) * 8 + cz, "grp": grp} for j in (2, 1, 3)]
    along_z = [{"brick": cy * 8 + (cz + j) % 8, "grp": grp} for j in (4, 3, 5, 2, 6, 1, 7)]

    def load(n, a, b):
        return pltpu.make_async_copy(a, b, load_sem.at[n])

    loads = [
        load(0, cond_h, cond), load(1, phase_h, phase), load(2, src_h, r),
        load(3, cinv_h, cinv.at[1]), load(4, inter_h, inter), load(5, adm_h, adm),
    ]
    for copy in loads:
        copy.start()
    barrier = pltpu.get_barrier_semaphore()
    greeted = along_z + group + along_y + [up, down]
    for dev in greeted:
        pl.semaphore_signal(barrier, inc=1, device_id=dev, device_id_type=MESH)

    lane = lax.broadcasted_iota(jnp.int32, (8, LANES), 1)
    sub = lax.broadcasted_iota(jnp.int32, (8, LANES), 0)
    slab_row = lax.broadcasted_iota(jnp.int32, (CY, NZ), 0)
    slab_col = lax.broadcasted_iota(jnp.int32, (CY, NZ), 1)
    base = (brick % 4) * 32

    def remote(a, b, send, recv, dev):
        return pltpu.make_async_remote_copy(
            src_ref=a, dst_ref=b, send_sem=send, recv_sem=recv, device_id=dev, device_id_type=MESH
        )

    def await_bytes(ref, sem):
        pltpu.make_async_copy(ref, ref, sem).wait()

    depth = lax.broadcasted_iota(jnp.int32, (KB, NZ), 1)
    slab = lax.broadcasted_iota(jnp.int32, (KB, NZ), 0)
    start = jnp.int32(0)
    begins = jnp.zeros((KB, NZ), jnp.int32)
    ends = jnp.zeros((KB, NZ), jnp.int32)
    for k in range(KB):
        stop = start + ext[0, k]
        begins = jnp.where(slab == k, start, begins)
        ends = jnp.where(slab == k, stop, ends)
        start = stop
    own_onehot = jnp.where((depth >= begins) & (depth < ends), 1.0, 0.0).astype(F32)
    onehot[1] = own_onehot

    def restrict_row(planes):
        spread = jnp.zeros((8, LANES), F32)
        for f in range(4):
            total = jnp.sum(planes[f], axis=0, keepdims=True)
            value = jnp.sum(total * onehot[1], axis=1, keepdims=True)
            spread = spread + jnp.where(lane == base + 8 * f + sub, value, 0.0)
        return jnp.sum(spread, axis=0, keepdims=True) * (1.0 / SLAB_CELLS)

    loads[0].wait()
    loads[1].wait()

    def masked(x, carry):
        for i in range(2):
            value = cond[i, x] * jnp.where(phase[x] == i + 1, 1.0, LOW_COND)
            cd[i, x + 1] = value
            syc[0, i, pl.ds(x, 1), :] = value[0:1]
            syc[1, i, pl.ds(x, 1), :] = value[CY - 1 : CY]
        return carry

    lax.fori_loop(0, CX, masked, 0)

    loads[2].wait()

    def plane_of(x, carry):
        return tuple(carry[f] + r[f, x, 0:8] + r[f, x, 8:16] for f in range(4))

    planes = lax.fori_loop(0, CX, plane_of, tuple(jnp.zeros((8, NZ), F32) for _ in range(4)))
    row_g[0:1] = restrict_row(planes)
    loads[3].wait()

    pl.semaphore_wait(barrier, len(greeted))

    started = []

    def go(copy):
        copy.start()
        started.append(copy)
        return copy

    for dev in group:
        remote(row_g.at[pl.ds(0, 1)], slots_g.at[pl.ds(grp, 1)], p0_send.at[0], p0_recv.at[0], dev).start()
    pltpu.make_async_copy(row_g.at[pl.ds(0, 1)], slots_g.at[pl.ds(grp, 1)], p0_recv.at[0]).start()
    cond_up = go(remote(cd.at[:, CX], hxc.at[0], near_send.at[0], near_recv.at[0], up))
    cond_down = go(remote(cd.at[:, 1], hxc.at[1], near_send.at[1], near_recv.at[1], down))
    cond_right = go(remote(syc.at[1], hyc.at[0], near_send.at[2], near_recv.at[2], right))
    cond_left = go(remote(syc.at[0], hyc.at[1], near_send.at[3], near_recv.at[3], left))
    hot_up = go(remote(onehot.at[1], onehot.at[0], near_send.at[4], near_recv.at[4], up))
    hot_down = go(remote(onehot.at[1], onehot.at[2], near_send.at[5], near_recv.at[5], down))
    cinv_up = go(remote(cinv.at[1], cinv.at[0], near_send.at[6], near_recv.at[6], up))
    cinv_down = go(remote(cinv.at[1], cinv.at[2], near_send.at[7], near_recv.at[7], down))

    loads[4].wait()
    loads[5].wait()

    def rates(x, carry):
        mask = inter[x].astype(F32)
        cr[x] = adm[0, x] * mask
        sr[x] = adm[1, x] * mask
        return carry

    lax.fori_loop(0, CX, rates, 0)
    for f in range(4):
        for edge in (0, CX + 1):
            first[f, edge] = jnp.zeros((CY, NZ), F32)
            second[0, f, edge] = jnp.zeros((CY, NZ), F32)
            second[1, f, edge] = jnp.zeros((CY, NZ), F32)

    await_bytes(slots_g, p0_recv.at[0])
    row_g[8:9] = jnp.sum(slots_g[...], axis=0, keepdims=True)
    for dev in along_y:
        remote(row_g.at[pl.ds(8, 1)], slots_y.at[pl.ds(cy, 1)], p0_send.at[1], p0_recv.at[1], dev).start()
    pltpu.make_async_copy(row_g.at[pl.ds(8, 1)], slots_y.at[pl.ds(cy, 1)], p0_recv.at[1]).start()

    inside = [
        jnp.where(brick > 0, 1.0, 0.0).astype(F32), jnp.where(brick < 31, 1.0, 0.0).astype(F32),
        jnp.where(grp > 0, 1.0, 0.0).astype(F32), jnp.where(grp < 7, 1.0, 0.0).astype(F32),
    ]
    for copy in (cond_up, cond_down, cond_right, cond_left):
        copy.wait_recv()
    for i in range(2):
        cd[i, 0] = hxc[0, i] * inside[0]
        cd[i, CX + 1] = hxc[1, i] * inside[1]

    def weigh(x, carry):
        out_low = jnp.where((x == 0) & (brick == 0), 1.0, 0.0).astype(F32)
        out_high = jnp.where((x == CX - 1) & (brick == 31), 1.0, 0.0).astype(F32)
        charge = cr[x]
        for i in range(2):
            here = cd[i, x + 1]
            low = 0.5 * (here + cd[i, x])
            high = 0.5 * (here + cd[i, x + 2])
            before = hyc[0, i, pl.ds(x, 1), :] * inside[2]
            after = hyc[1, i, pl.ds(x, 1), :] * inside[3]
            ym = 0.5 * (here + jnp.where(slab_row == 0, before, roll(here, 1, 0)))
            yp = 0.5 * (here + jnp.where(slab_row == CY - 1, after, roll(here, -1, 0)))
            zm = 0.5 * (here + jnp.where(slab_col == 0, 0.0, roll(here, 1, 1)))
            zp = 0.5 * (here + jnp.where(slab_col == NZ - 1, 0.0, roll(here, -1, 1)))
            total = low + high + ym + yp + zm + zp + EPS_SHIFT
            tw[i, x] = total
            dinv[i, x] = 1.0 / (total + charge)
            ee[i, x] = (
                EPS_SHIFT + zm + zp + out_low * low + out_high * high
                + jnp.where(slab_row == 0, ym, 0.0) * (1.0 - inside[2])
                + jnp.where(slab_row == CY - 1, yp, 0.0) * (1.0 - inside[3])
            )
            wx[i, x] = low * (1.0 - out_low)
            wx[i, x + 1] = high * (1.0 - out_high)
            wyb[0, i, pl.ds(x, 1), :] = ym[0:1] * inside[2]
            wyb[1, i, pl.ds(x, 1), :] = yp[CY - 1 : CY] * inside[3]
            wym[i, x] = jnp.where(slab_row == 0, 0.0, ym)
            wyp[i, x] = jnp.where(slab_row == CY - 1, 0.0, yp)
            wzm[i, x] = jnp.where(slab_col == 0, 0.0, zm)
            wzp[i, x] = jnp.where(slab_col == NZ - 1, 0.0, zp)
        return carry

    lax.fori_loop(0, CX, weigh, 0)

    def around(v, f, x, center):
        i = f // 2
        return (
            wx[i, x] * v[f, x] + wx[i, x + 1] * v[f, x + 2]
            + wym[i, x] * roll(center, 1, 0) + wyp[i, x] * roll(center, -1, 0)
            + wzm[i, x] * roll(center, 1, 1) + wzp[i, x] * roll(center, -1, 1)
        )

    def smooth(given, k):
        out = second.at[k % 2]

        def scaled(x, carry):
            for f in range(4):
                first[f, x + 1] = given[f, x] * dinv[f // 2, x]
            return carry

        lax.fori_loop(0, CX, scaled, 0)

        def stencil(x, carry):
            v = [first[f, x + 1] for f in range(4)]
            real, imag = sr[x] * (v[0] - v[2]), sr[x] * (v[1] - v[3])
            swirl = (imag, -real, -imag, real)
            for f in range(4):
                value = v[f] + dinv[f // 2, x] * (around(first, f, x, v[f]) + cr[x] * v[f ^ 2] + swirl[f])
                out[f, x + 1] = value
                sy[k, 0, f, pl.ds(x, 1), :] = value[0:1]
                sy[k, 1, f, pl.ds(x, 1), :] = value[CY - 1 : CY]
            return carry

        lax.fori_loop(0, 2, lambda n, c: stencil(n * (CX - 1), c), 0)
        halos = [
            remote(out.at[:, CX], hx.at[k, 0], halo_sem.at[k, 0, 0], halo_sem.at[k, 1, 0], up),
            remote(out.at[:, 1], hx.at[k, 1], halo_sem.at[k, 0, 1], halo_sem.at[k, 1, 1], down),
        ]
        for copy in halos:
            copy.start()
        lax.fori_loop(1, CX - 1, stencil, 0)
        sides = [
            remote(sy.at[k, 1], hy.at[k, 0], halo_sem.at[k, 0, 2], halo_sem.at[k, 1, 2], right),
            remote(sy.at[k, 0], hy.at[k, 1], halo_sem.at[k, 0, 3], halo_sem.at[k, 1, 3], left),
        ]
        for copy in sides:
            copy.start()
        return halos + sides

    def operate(k):
        v = second.at[k % 2]

        def stencil(x, carry):
            c = [v[f, x + 1] for f in range(4)]
            over_real, over_imag = c[0] - c[2], c[1] - c[3]
            real = cr[x] * over_real - sr[x] * over_imag
            imag = cr[x] * over_imag + sr[x] * over_real
            flow = (real, imag, -real, -imag)
            for f in range(4):
                u[f, x] = tw[f // 2, x] * c[f] - around(v, f, x, c[f]) + flow[f]
            return carry

        lax.fori_loop(0, CX, stencil, 0)

    def receive_halos(k, copies):
        for copy in copies:
            copy.wait_recv()
        for f in range(4):
            u[f, 0] = u[f, 0] - wx[f // 2, 0] * hx[k, 0, f]
            u[f, CX - 1] = u[f, CX - 1] - wx[f // 2, CX] * hx[k, 1, f]

        def rows(x, carry):
            for f in range(4):
                for side, y in ((0, 0), (1, CY - 1)):
                    u[f, x, y : y + 1, :] = u[f, x, y : y + 1, :] - (
                        wyb[side, f // 2, pl.ds(x, 1), :] * hy[k, side, f, pl.ds(x, 1), :]
                    )
            return carry

        lax.fori_loop(0, CX, rows, 0)
        for copy in copies:
            copy.wait_send()

    def correct(coarse):
        profile = []
        for j in range(3):
            per_field = []
            for f in range(4):
                product = jnp.zeros((8, LANES), F32)
                for s in range(8):
                    product = product + cinv[j, 8 * f : 8 * f + 8, LANES * s : LANES * s + LANES] * coarse[s]
                value = jnp.sum(product, axis=1, keepdims=True)
                per_field.append(jnp.sum(value * onehot[j], axis=0, keepdims=True))
            profile.append(per_field)
        own = profile[1]
        rows = own + [roll(own[f], 1, 1) for f in range(4)] + [roll(own[f], -1, 1) for f in range(4)]
        rows = rows + [own[0] - own[2], own[1] - own[3]]
        for n, value in enumerate(rows):
            table[n] = jnp.broadcast_to(value, (8, NZ))
        for f in range(4):
            u[f, 0] = u[f, 0] - wx[f // 2, 0] * (profile[0][f] - own[f])
            u[f, CX - 1] = u[f, CX - 1] - wx[f // 2, CX] * (profile[2][f] - own[f])

    def advance(k, alpha):
        zero = jnp.zeros((8, LANES), F32)
        ri, ii = zero, zero
        planes = [[] for _ in range(4)]
        for t in range(TILES):
            lanes = slice(LANES * t, LANES * (t + 1))
            p = [table[n, :, lanes] for n in range(14)]

            def step(x, carry):
                ri, ii, *sums = carry
                for half in range(2):
                    at = (x, slice(8 * half, 8 * half + 8), lanes)
                    charge, storage = cr[at], sr[at]
                    real = charge * p[12] - storage * p[13]
                    imag = charge * p[13] + storage * p[12]
                    flow = (real, imag, -real, -imag)
                    for f in range(4):
                        i = f // 2
                        raised = u[(f,) + at] + (
                            ee[(i,) + at] * p[f] - wzm[(i,) + at] * p[4 + f] - wzp[(i,) + at] * p[8 + f] + flow[f]
                        )
                        left_over = r[(f,) + at]
                        if k > 0:
                            old = q[(f,) + at]
                            left_over = left_over - alpha * old
                            r[(f,) + at] = left_over
                            raised = old - alpha * raised
                        q[(f,) + at] = raised
                        ri = ri + left_over * raised
                        ii = ii + raised * raised
                        sums[f] = sums[f] + raised
                return (ri, ii, *sums)

            ri, ii, *sums = lax.fori_loop(0, CX, step, (ri, ii, zero, zero, zero, zero))
            for f in range(4):
                planes[f].append(sums[f])
        return ri, ii, [jnp.concatenate(parts, axis=1) for parts in planes]

    def update_search(k, alpha):
        smoothed = second.at[k % 2]

        def step(x, carry):
            for f in range(4):
                put = smoothed[f, x + 1] + jnp.concatenate([table[f], table[f]], axis=0)
                if k == 0:
                    z[f, x] = put
                else:
                    old = z[f, x]
                    sol[f, x] = alpha * old if k == 1 else sol[f, x] + alpha * old
                    z[f, x] = old - alpha * put
            return carry

        lax.fori_loop(0, CX, step, 0)

    slot = cx * 32 + (cz % 4) * 8 + (cz // 4) * 4 + cy
    ys = [((cy + j) % 4) * 8 for j in range(4)]
    xs = [((cx + j) % 4) * 2 + core for j in range(4)]
    far_first = [2, 1, 3, 0]
    plane_order = [(dy, dx) for dy in far_first for dx in far_first]
    plane_order.sort(key=lambda p: -min(p[0], 4 - p[0]) - min(p[1], 4 - p[1]))
    sibling = {"brick": brick, "grp": cx * 2 + 1 - core}

    def share(k, ri, ii, planes):
        coarse = restrict_row(planes)
        ri = jnp.sum(jnp.sum(ri, axis=0, keepdims=True), axis=1, keepdims=True)
        ii = jnp.sum(jnp.sum(ii, axis=0, keepdims=True), axis=1, keepdims=True)
        row_c[k, 0:1, 0:LANES] = coarse
        row_c[k, 0:1, LANES : 2 * LANES] = jnp.where(lane[0:1] < 64, ri, ii)
        copy = remote(row_c.at[k], slots_c.at[k], core_sem.at[k, 0], core_sem.at[k, 1], sibling)
        copy.start()
        copy.wait_recv()
        both = row_c[k, 0:1] + slots_c[k, 0:1]
        row_all[k, 0:1] = both

        def send(by, bx):
            remote(
                row_all.at[k, pl.ds(0, 1)], slots_all.at[k, pl.ds(slot, 1)], all_send.at[k], all_recv.at[k],
                {"brick": by, "grp": bx},
            ).start()

        def far(n, carry):
            half = (n + 1) // 2
            dz = 4 + half * (1 - 2 * (n % 2))
            bz = (cz + dz) % 8
            for dy, dx in plane_order:
                send(ys[dy] + bz, xs[dx])
            return carry

        lax.fori_loop(0, 7, far, 0)
        for dy, dx in plane_order[:-1]:
            send(ys[dy] + cz, xs[dx])
        pltpu.make_async_copy(
            row_all.at[k, pl.ds(0, 1)], slots_all.at[k, pl.ds(slot, 1)], all_recv.at[k]
        ).start()
        return copy

    def gather(k):
        await_bytes(slots_all.at[k], all_recv.at[k])
        rows = slots_all[k, 0:8]
        for n in range(1, 16):
            rows = rows + slots_all[k, 8 * n : 8 * n + 8]
        dots = jnp.sum(rows[:, LANES:], axis=0, keepdims=True)
        other = roll(dots, 64, 1)
        ri = jnp.where(lane[0:1] < 64, dots, other)
        ii = jnp.where(lane[0:1] < 64, other, dots)
        return rows[:, :LANES], ri / (ii + 1e-6)

    def coarse_rows(rows):
        return [rows[4 * (s % 2) + s // 2 : 4 * (s % 2) + s // 2 + 1] for s in range(8)]

    halos = smooth(r, 0)

    await_bytes(slots_y, p0_recv.at[1])
    slots_z[pl.ds(cz, 1)] = slots_y[...][None]
    for dev in along_z:
        remote(slots_y, slots_z.at[cz], p0_send.at[2], p0_recv.at[2], dev).start()

    operate(0)
    receive_halos(0, halos)
    for copy in (hot_up, hot_down, cinv_up, cinv_down):
        copy.wait_recv()
    await_bytes(slots_z.at[pl.ds(0, 7)], p0_recv.at[2])
    low = slots_z[0] + slots_z[1] + slots_z[2] + slots_z[3]
    high = slots_z[4] + slots_z[5] + slots_z[6] + slots_z[7]
    rows = jnp.concatenate([low, high], axis=0)
    alpha = None
    cores = []
    for k in range(ITERS):
        correct(coarse_rows(rows))
        ri, ii, planes = advance(k, None if k == 0 else jnp.broadcast_to(alpha, (8, LANES)))
        cores.append(share(k, ri, ii, planes))
        wide = None if k == 0 else jnp.broadcast_to(jnp.concatenate([alpha] * TILES, axis=1), (CY, NZ))
        if k < ITERS - 1:
            halos = smooth(q, k + 1)
        update_search(k, wide)
        if k < ITERS - 1:
            operate(k + 1)
            receive_halos(k + 1, halos)
        rows, alpha = gather(k)

    wide = jnp.broadcast_to(jnp.concatenate([alpha] * TILES, axis=1), (CY, NZ))

    def finish(x, carry):
        for f in range(4):
            sol[f, x] = sol[f, x] + wide * z[f, x]
            r[f, x] = r[f, x] - wide * q[f, x]
        return carry

    lax.fori_loop(0, CX, finish, 0)
    outs = [pltpu.make_async_copy(sol, sol_h, out_sem.at[0]), pltpu.make_async_copy(r, res_h, out_sem.at[1])]
    for copy in outs:
        copy.start()
    for copy in started + cores:
        copy.wait_send()
    await_bytes(sizes.at[pl.ds(0, 7), :, pl.ds(0, LANES)], p0_send.at[0])
    await_bytes(sizes.at[pl.ds(0, 3), :, pl.ds(0, LANES)], p0_send.at[1])
    await_bytes(slots_z.at[pl.ds(0, 7)], p0_send.at[2])
    for k in range(ITERS):
        await_bytes(sizes, all_send.at[k])
    for copy in outs:
        copy.wait()


def local(source, phase_label, interface, conductivity, admittance, extents, coarse_inverse):
    block = (CX, CY, NZ)
    padded = (CX + 2, CY, NZ)
    vmem = lambda *shape: pltpu.VMEM(shape, F32)
    ints = pltpu.VMEM(block, jnp.int32)
    dma = lambda *shape: pltpu.SemaphoreType.DMA(shape)
    scratch = [
        vmem(4, *block), vmem(4, *block), vmem(4, *block), vmem(4, *block), vmem(4, *block),
        vmem(4, *padded), vmem(2, 4, *padded), vmem(2, *block), ints, ints, vmem(2, *block),
        vmem(2, *padded), vmem(*block), vmem(*block),
        vmem(2, CX + 1, CY, NZ), vmem(2, *block), vmem(2, *block), vmem(2, *block), vmem(2, *block),
        vmem(2, *block), vmem(2, *block), vmem(2, *block), vmem(2, 2, CX, NZ),
        vmem(3, 4 * KB, 1024), vmem(3, KB, NZ), vmem(14, 8, NZ),
        vmem(2, 2, CY, NZ), vmem(2, 2, CX, NZ), vmem(2, 2, CX, NZ),
        vmem(3, 2, 4, CY, NZ), vmem(3, 2, 4, CX, NZ), vmem(3, 2, 4, CX, NZ),
        vmem(16, LANES), vmem(8, LANES), vmem(4, LANES), vmem(8, 4, LANES),
        vmem(3, 1, 2 * LANES), vmem(3, 1, 2 * LANES), vmem(3, 1, 2 * LANES), vmem(3, 128, 2 * LANES),
        vmem(127, 1, 2 * LANES),
        dma(6), dma(2), dma(8), dma(8), dma(1), dma(3, 2, 4), dma(3), dma(3), dma(3, 2), dma(3), dma(3),
    ]
    hbm = pl.BlockSpec(memory_space=pl.ANY)
    out = jax.ShapeDtypeStruct((4, *block), F32)
    return pl.pallas_call(
        kernel,
        out_shape=(out, out),
        in_specs=[pl.BlockSpec(memory_space=pltpu.SMEM)] + [hbm] * 6,
        out_specs=(hbm, hbm),
        scratch_shapes=scratch,
        compiler_params=pltpu.CompilerParams(
            collective_id=0, has_side_effects=True, vmem_limit_bytes=48 * 1024 * 1024
        ),
    )(extents, source, phase_label, interface, conductivity, admittance, coarse_inverse)


def solution(mesh):
    placed = (
        P(None, "brick", "grp", None),
        P("brick", "grp", None),
        P("brick", "grp", None),
        P(None, "brick", "grp", None),
        P(None, "brick", "grp", None),
        P("brick", None),
        P("brick", None),
    )
    return jax.shard_map(
        local,
        mesh=mesh,
        in_specs=placed,
        out_specs=(P(None, "brick", "grp", None), P(None, "brick", "grp", None)),
        check_vma=False,
    )
```

time: 517 us -> 65.9 us (0.13)
  blocking collectives: 356 us -> 0 us
  starting transfers between devices: 69.4 us -> 0 us
  Pallas kernels: 0 us -> 56.2 us
  other arithmetic: 45.7 us -> 0 us
  waiting for transfers between devices: 23.5 us -> 0 us
    psum x6 -> x0, blocking collectives: 268 us -> none  [the longest x3 230 us: local(): lax.psum((jnp.sum(residual * image), jnp.sum(image * image)), ('brick', '...]
    all_gather x3 -> x0, blocking collectives: 87.7 us -> none  [local(): full_coarse = lax.all_gather(group_sum, 'brick', axis=0, tiled=True)]
    ppermute x16 -> x0, starting transfers between devices: 69.4 us -> none  [the longest x8 50.4 us: padded_2(): before = lax.ppermute(last, axis, up)]
    pallas_call x0 -> x1, Pallas kernels: none -> 56.2 us  [local(): pl.pallas_call(kernel, out_shape=(out, out), in_specs=[pl.BlockSpec(memor...]
    ppermute x16 -> x0, waiting for transfers between devices: 23.5 us -> none  [the longest x8 22 us: padded_2(): after = lax.ppermute(first, axis, down)]
    add x4 -> x0, other arithmetic: 19.9 us -> none  [the longest x3 16.9 us: local(): search = second + profile[:, None, None, :]]
    reduce_sum x6 -> x0, other arithmetic: 13.3 us -> none  [the longest x3 9.77 us: local(): jnp.sum(image * image)]
    slice x9 -> x0, local copies, waits for them, and re-layouts: 6.35 us -> none  [the longest x6 6.3 us: shifted(): lax.slice_in_dim(values, 0, count - 1, axis=along)]
  transfers between devices with their start and end apart: 16 -> 0, of which waited for: 11 -> 0; matrix products, arithmetic and copies ran while one was open for 0% -> 0% of each run, Pallas kernels for 0% -> 0%
where the time goes in v1:
time: 65.9 us; the launch traced here: 65.6 us
  Pallas kernels  56.2 us (85%)
  local copies, waits for them, and re-layouts  8.7 us (13%)
  between operations  0.66 us (1%)
    pallas_call x1, Pallas kernels, local(): pl.pallas_call(kernel, out_shape=(out, out), in_specs=[pl.BlockSpec(memor...  56.2 us
    unnamed x16, local copies, waits for them, and re-layouts  8.7 us

profile of v1, /device:TPU:1, one launch (start us, length us, event | category | flops | bytes accessed | tf_op | source)
XLA Modules:
  0.0 65.6 jit_solution(18385966690292926828)
XLA Ops:
  0.6 0.0 copy-start
  0.6 1.2 %copy-done = f32[4,8,16,512]{3,2,1,0:T(8,128)S(1)} copy-done((f32[4,8,16,512]{3,2,1,0:T(8,128)S(1)}, f32[4,8,16,512]{3,2,1,0:T(8,128)}, u32[]{:S(2)}) %copy-start) | copy-done | bytes 1048600
  1.9 0.0 copy-start.1
  1.9 1.0 %copy-done.1 = f32[2,8,16,512]{3,2,1,0:T(8,128)S(1)} copy-done((f32[2,8,16,512]{3,2,1,0:T(8,128)S(1)}, f32[2,8,16,512]{3,2,1,0:T(8,128)}, u32[]{:S(2)}) %copy-start.1) | copy-done | bytes 524312
  2.9 0.0 copy-start.2
  2.9 1.0 %copy-done.2 = f32[2,8,16,512]{3,2,1,0:T(8,128)S(1)} copy-done((f32[2,8,16,512]{3,2,1,0:T(8,128)S(1)}, f32[2,8,16,512]{3,2,1,0:T(8,128)}, u32[]{:S(2)}) %copy-start.2) | copy-done | bytes 524312
  3.9 0.0 copy-start.3
  3.9 0.9 %copy-done.3 = s32[8,16,512]{2,1,0:T(8,128)S(1)} copy-done((s32[8,16,512]{2,1,0:T(8,128)S(1)}, s32[8,16,512]{2,1,0:T(8,128)}, u32[]{:S(2)}) %copy-start.3) | copy-done | bytes 262168
  4.9 0.0 copy-start.4
  4.9 0.9 %copy-done.4 = s32[8,16,512]{2,1,0:T(8,128)S(1)} copy-done((s32[8,16,512]{2,1,0:T(8,128)S(1)}, s32[8,16,512]{2,1,0:T(8,128)}, u32[]{:S(2)}) %copy-start.4) | copy-done | bytes 262168
  5.8 0.0 copy-start.5
  5.8 0.9 %copy-done.5 = f32[32,1024]{1,0:T(8,128)S(1)} copy-done((f32[32,1024]{1,0:T(8,128)S(1)}, f32[32,1024]{1,0:T(8,128)}, u32[]{:S(2)}) %copy-start.5) | copy-done | bytes 131096
  6.7 0.0 copy-start.6
  6.8 0.7 copy-done.6
  7.4 56.2 %shard_map.86 = (f32[4,8,16,512]{3,2,1,0:T(8,128)S(1)}, f32[4,8,16,512]{3,2,1,0:T(8,128)S(1)}) custom-call(s32[1,8]{1,0:T(1,128)S(1)} %copy-done.6, f32[4,8,16,512]{3,2,1,0:T(8,128)S(1)} %copy-done, s32[8,16,512]{2,1,0:T(8,128)S(1)} %copy-done.3, s32[8,16,512]{2,1,0:T(8,128)S(1)} %copy-done.4, f32[2,8,16,512]{3,2,1,0:T(8,128)S(1)} %copy-done.1, ...), custom_call_target="tpu_custom_call" | custom-call | tf_op jit(solution)/shard_map/pallas_call | solution.py:482
  63.7 1.0 %copy.11 = f32[4,8,16,512]{3,2,1,0:T(8,128)} copy(f32[4,8,16,512]{3,2,1,0:T(8,128)S(1)} %get-tuple-element.4) | data formatting | bytes 2097152
  64.6 1.0 %copy.12 = f32[4,8,16,512]{3,2,1,0:T(8,128)} copy(f32[4,8,16,512]{3,2,1,0:T(8,128)S(1)} %get-tuple-element.5) | data formatting | bytes 2097152
Async XLA Ops:
  0.6 1.2 %copy-start = (f32[4,8,16,512]{3,2,1,0:T(8,128)S(1)}, f32[4,8,16,512]{3,2,1,0:T(8,128)}, u32[]{:S(2)}) copy-start(f32[4,8,16,512]{3,2,1,0:T(8,128)} %src_h.1) | copy-start | bytes 3145732
  1.9 1.0 %copy-start.1 = (f32[2,8,16,512]{3,2,1,0:T(8,128)S(1)}, f32[2,8,16,512]{3,2,1,0:T(8,128)}, u32[]{:S(2)}) copy-start(f32[2,8,16,512]{3,2,1,0:T(8,128)} %cond_h.1) | copy-start | bytes 1572868
  2.9 1.0 %copy-start.2 = (f32[2,8,16,512]{3,2,1,0:T(8,128)S(1)}, f32[2,8,16,512]{3,2,1,0:T(8,128)}, u32[]{:S(2)}) copy-start(f32[2,8,16,512]{3,2,1,0:T(8,128)} %adm_h.1) | copy-start | bytes 1572868
  3.9 0.9 %copy-start.3 = (s32[8,16,512]{2,1,0:T(8,128)S(1)}, s32[8,16,512]{2,1,0:T(8,128)}, u32[]{:S(2)}) copy-start(s32[8,16,512]{2,1,0:T(8,128)} %phase_h.1) | copy-start | bytes 786436
  4.9 0.9 %copy-start.4 = (s32[8,16,512]{2,1,0:T(8,128)S(1)}, s32[8,16,512]{2,1,0:T(8,128)}, u32[]{:S(2)}) copy-start(s32[8,16,512]{2,1,0:T(8,128)} %inter_h.1) | copy-start | bytes 786436
  5.8 0.9 %copy-start.5 = (f32[32,1024]{1,0:T(8,128)S(1)}, f32[32,1024]{1,0:T(8,128)}, u32[]{:S(2)}) copy-start(f32[32,1024]{1,0:T(8,128)} %cinv_h.1) | copy-start | bytes 393220
  6.7 0.7 copy-start.6

commit v2 on v1

--- a/solution.py
+++ b/solution.py
@@ -24,7 +24,7 @@
     ext, src_h, phase_h, inter_h, cond_h, adm_h, cinv_h, sol_h, res_h,
     r, q, u, z, sol, first, second, cond, phase, inter, adm, cd, cr, sr,
     wx, wym, wyp, wzm, wzp, tw, ee, dinv, wyb, cinv, onehot, table,
-    hxc, hyc, syc, hx, hy, sy, row_g, slots_g, slots_y, slots_z, row_c, slots_c, row_all, slots_all, sizes,
+    hxc, hyc, syc, hx, hy, sy, row_z, slots_z, row_p, slots_p, row_c, slots_c, row_all, slots_all, sizes,
     load_sem, out_sem, near_send, near_recv, c_sem, halo_sem, p0_send, p0_recv, core_sem, all_send, all_recv,
 ):
     brick, grp = lax.axis_index("brick"), lax.axis_index("grp")
@@ -33,8 +33,14 @@
     down = {"brick": (brick + 31) % 32, "grp": grp}
     right = {"brick": brick, "grp": (grp + 1) % 8}
     left = {"brick": brick, "grp": (grp + 7) % 8}
-    group = [{"brick": brick, "grp": (grp + j) % 8} for j in (4, 5, 3, 2, 6, 1, 7)]
-    along_y = [{"brick": ((cy + j) % 4) * 8 + cz, "grp": grp} for j in (2, 1, 3)]
+    ys = [((cy + j) % 4) * 8 for j in range(4)]
+    xs = [((cx + j) % 4) * 2 for j in range(4)]
+    far_first = [(dy, dx) for dy in (2, 1, 3, 0) for dx in (2, 1, 3, 0)]
+    far_first.sort(key=lambda p: -min(p[0], 4 - p[0]) - min(p[1], 4 - p[1]))
+    plane = [
+        {"brick": ys[dy] + cz, "grp": xs[dx] + (core if same else 1 - core)}
+        for dy, dx in far_first for same in (0, 1) if (dy, dx, same) != (0, 0, 1)
+    ]
     along_z = [{"brick": cy * 8 + (cz + j) % 8, "grp": grp} for j in (4, 3, 5, 2, 6, 1, 7)]
 
     def load(n, a, b):
@@ -47,7 +53,7 @@
     for copy in loads:
         copy.start()
     barrier = pltpu.get_barrier_semaphore()
-    greeted = along_z + group + along_y + [up, down]
+    greeted = along_z + plane + [up, down]
     for dev in greeted:
         pl.semaphore_signal(barrier, inc=1, device_id=dev, device_id_type=MESH)
 
@@ -55,7 +61,7 @@
     sub = lax.broadcasted_iota(jnp.int32, (8, LANES), 0)
     slab_row = lax.broadcasted_iota(jnp.int32, (CY, NZ), 0)
     slab_col = lax.broadcasted_iota(jnp.int32, (CY, NZ), 1)
-    base = (brick % 4) * 32
+    base = (cz % 4) * 32
 
     def remote(a, b, send, recv, dev):
         return pltpu.make_async_remote_copy(
@@ -78,7 +84,7 @@
     own_onehot = jnp.where((depth >= begins) & (depth < ends), 1.0, 0.0).astype(F32)
     onehot[1] = own_onehot
 
-    def restrict_row(planes):
+    def restrict_row(planes, base):
         spread = jnp.zeros((8, LANES), F32)
         for f in range(4):
             total = jnp.sum(planes[f], axis=0, keepdims=True)
@@ -105,7 +111,7 @@
         return tuple(carry[f] + r[f, x, 0:8] + r[f, x, 8:16] for f in range(4))
 
     planes = lax.fori_loop(0, CX, plane_of, tuple(jnp.zeros((8, NZ), F32) for _ in range(4)))
-    row_g[0:1] = restrict_row(planes)
+    row_z[...] = restrict_row(planes, base)
     loads[3].wait()
 
     pl.semaphore_wait(barrier, len(greeted))
@@ -117,9 +123,9 @@
         started.append(copy)
         return copy
 
-    for dev in group:
-        remote(row_g.at[pl.ds(0, 1)], slots_g.at[pl.ds(grp, 1)], p0_send.at[0], p0_recv.at[0], dev).start()
-    pltpu.make_async_copy(row_g.at[pl.ds(0, 1)], slots_g.at[pl.ds(grp, 1)], p0_recv.at[0]).start()
+    for dev in along_z:
+        remote(row_z, slots_z.at[pl.ds(cz, 1)], p0_send.at[0], p0_recv.at[0], dev).start()
+    pltpu.make_async_copy(row_z, slots_z.at[pl.ds(cz, 1)], p0_recv.at[0]).start()
     cond_up = go(remote(cd.at[:, CX], hxc.at[0], near_send.at[0], near_recv.at[0], up))
     cond_down = go(remote(cd.at[:, 1], hxc.at[1], near_send.at[1], near_recv.at[1], down))
     cond_right = go(remote(syc.at[1], hyc.at[0], near_send.at[2], near_recv.at[2], right))
@@ -144,12 +150,6 @@
             first[f, edge] = jnp.zeros((CY, NZ), F32)
             second[0, f, edge] = jnp.zeros((CY, NZ), F32)
             second[1, f, edge] = jnp.zeros((CY, NZ), F32)
-
-    await_bytes(slots_g, p0_recv.at[0])
-    row_g[8:9] = jnp.sum(slots_g[...], axis=0, keepdims=True)
-    for dev in along_y:
-        remote(row_g.at[pl.ds(8, 1)], slots_y.at[pl.ds(cy, 1)], p0_send.at[1], p0_recv.at[1], dev).start()
-    pltpu.make_async_copy(row_g.at[pl.ds(8, 1)], slots_y.at[pl.ds(cy, 1)], p0_recv.at[1]).start()
 
     inside = [
         jnp.where(brick > 0, 1.0, 0.0).astype(F32), jnp.where(brick < 31, 1.0, 0.0).astype(F32),
@@ -193,7 +193,8 @@
             wzp[i, x] = jnp.where(slab_col == NZ - 1, 0.0, zp)
         return carry
 
-    lax.fori_loop(0, CX, weigh, 0)
+    ends = lambda n: n + 4 * (n // 2)
+    lax.fori_loop(0, 4, lambda n, c: weigh(ends(n), c), 0)
 
     def around(v, f, x, center):
         i = f // 2
@@ -203,15 +204,13 @@
             + wzm[i, x] * roll(center, 1, 1) + wzp[i, x] * roll(center, -1, 1)
         )
 
-    def smooth(given, k):
+    def smooth(given, k, between):
         out = second.at[k % 2]
 
         def scaled(x, carry):
             for f in range(4):
                 first[f, x + 1] = given[f, x] * dinv[f // 2, x]
             return carry
-
-        lax.fori_loop(0, CX, scaled, 0)
 
         def stencil(x, carry):
             v = [first[f, x + 1] for f in range(4)]
@@ -224,6 +223,7 @@
                 sy[k, 1, f, pl.ds(x, 1), :] = value[CY - 1 : CY]
             return carry
 
+        lax.fori_loop(0, 4, lambda n, c: scaled(ends(n), c), 0)
         lax.fori_loop(0, 2, lambda n, c: stencil(n * (CX - 1), c), 0)
         halos = [
             remote(out.at[:, CX], hx.at[k, 0], halo_sem.at[k, 0, 0], halo_sem.at[k, 1, 0], up),
@@ -231,6 +231,8 @@
         ]
         for copy in halos:
             copy.start()
+        between()
+        lax.fori_loop(2, CX - 2, scaled, 0)
         lax.fori_loop(1, CX - 1, stencil, 0)
         sides = [
             remote(sy.at[k, 1], hy.at[k, 0], halo_sem.at[k, 0, 2], halo_sem.at[k, 1, 2], right),
@@ -348,29 +350,22 @@
 
         lax.fori_loop(0, CX, step, 0)
 
-    slot = cx * 32 + (cz % 4) * 8 + (cz // 4) * 4 + cy
-    ys = [((cy + j) % 4) * 8 for j in range(4)]
-    xs = [((cx + j) % 4) * 2 + core for j in range(4)]
-    far_first = [2, 1, 3, 0]
-    plane_order = [(dy, dx) for dy in far_first for dx in far_first]
-    plane_order.sort(key=lambda p: -min(p[0], 4 - p[0]) - min(p[1], 4 - p[1]))
+    slot = (cz % 4) * 32 + cx * 8 + cy * 2 + cz // 4
     sibling = {"brick": brick, "grp": cx * 2 + 1 - core}
 
     def share(k, ri, ii, planes):
-        coarse = restrict_row(planes)
+        coarse = restrict_row(planes, 0)
         ri = jnp.sum(jnp.sum(ri, axis=0, keepdims=True), axis=1, keepdims=True)
         ii = jnp.sum(jnp.sum(ii, axis=0, keepdims=True), axis=1, keepdims=True)
-        row_c[k, 0:1, 0:LANES] = coarse
-        row_c[k, 0:1, LANES : 2 * LANES] = jnp.where(lane[0:1] < 64, ri, ii)
+        row_c[k] = jnp.where(lane[0:1] < 32, coarse, jnp.where(lane[0:1] < 64, ri, ii))
         copy = remote(row_c.at[k], slots_c.at[k], core_sem.at[k, 0], core_sem.at[k, 1], sibling)
         copy.start()
         copy.wait_recv()
-        both = row_c[k, 0:1] + slots_c[k, 0:1]
-        row_all[k, 0:1] = both
+        row_all[k] = row_c[k] + slots_c[k]
 
         def send(by, bx):
             remote(
-                row_all.at[k, pl.ds(0, 1)], slots_all.at[k, pl.ds(slot, 1)], all_send.at[k], all_recv.at[k],
+                row_all.at[k], slots_all.at[k, pl.ds(slot, 1)], all_send.at[k], all_recv.at[k],
                 {"brick": by, "grp": bx},
             ).start()
 
@@ -378,79 +373,80 @@
             half = (n + 1) // 2
             dz = 4 + half * (1 - 2 * (n % 2))
             bz = (cz + dz) % 8
-            for dy, dx in plane_order:
-                send(ys[dy] + bz, xs[dx])
+            for dy, dx in far_first:
+                send(ys[dy] + bz, xs[dx] + core)
             return carry
 
         lax.fori_loop(0, 7, far, 0)
-        for dy, dx in plane_order[:-1]:
-            send(ys[dy] + cz, xs[dx])
+        for dy, dx in far_first[:-1]:
+            send(ys[dy] + cz, xs[dx] + core)
         pltpu.make_async_copy(
-            row_all.at[k, pl.ds(0, 1)], slots_all.at[k, pl.ds(slot, 1)], all_recv.at[k]
+            row_all.at[k], slots_all.at[k, pl.ds(slot, 1)], all_recv.at[k]
         ).start()
         return copy
 
     def gather(k):
         await_bytes(slots_all.at[k], all_recv.at[k])
-        rows = slots_all[k, 0:8]
-        for n in range(1, 16):
-            rows = rows + slots_all[k, 8 * n : 8 * n + 8]
-        dots = jnp.sum(rows[:, LANES:], axis=0, keepdims=True)
-        other = roll(dots, 64, 1)
-        ri = jnp.where(lane[0:1] < 64, dots, other)
-        ii = jnp.where(lane[0:1] < 64, other, dots)
-        return rows[:, :LANES], ri / (ii + 1e-6)
-
-    def coarse_rows(rows):
-        return [rows[4 * (s % 2) + s // 2 : 4 * (s % 2) + s // 2 + 1] for s in range(8)]
-
-    halos = smooth(r, 0)
-
-    await_bytes(slots_y, p0_recv.at[1])
-    slots_z[pl.ds(cz, 1)] = slots_y[...][None]
-    for dev in along_z:
-        remote(slots_y, slots_z.at[cz], p0_send.at[2], p0_recv.at[2], dev).start()
-
+        quarters = []
+        for n in range(4):
+            rows = slots_all[k, 32 * n : 32 * n + 8]
+            for m in range(1, 4):
+                rows = rows + slots_all[k, 32 * n + 8 * m : 32 * n + 8 * m + 8]
+            quarters.append(rows)
+        dots = jnp.sum(quarters[0] + quarters[1] + quarters[2] + quarters[3], axis=0, keepdims=True)
+        alpha = (roll(dots, 64, 1) / (dots + 1e-6))[:, LANES - 1 :]
+        quarters = [jnp.where(lane < 32, rows, 0.0) for rows in quarters]
+        rows = quarters[0] + roll(quarters[1], 32, 1) + roll(quarters[2], 64, 1) + roll(quarters[3], 96, 1)
+        return [rows[s : s + 1] for s in range(8)], jnp.broadcast_to(alpha, (1, LANES))
+
+    def pass_on():
+        await_bytes(slots_z, p0_recv.at[0])
+        row_p[0] = jnp.sum(slots_z[0:4], axis=0, keepdims=True)
+        row_p[1] = jnp.sum(slots_z[4:8], axis=0, keepdims=True)
+        mine = slots_p.at[pl.ds(2 * cy, 2), pl.ds(grp, 1)]
+        for dev in plane:
+            remote(row_p, mine, p0_send.at[1], p0_recv.at[1], dev).start()
+        pltpu.make_async_copy(row_p, mine, p0_recv.at[1]).start()
+        lax.fori_loop(2, CX - 2, weigh, 0)
+
+    halos = smooth(r, 0, pass_on)
     operate(0)
     receive_halos(0, halos)
     for copy in (hot_up, hot_down, cinv_up, cinv_down):
         copy.wait_recv()
-    await_bytes(slots_z.at[pl.ds(0, 7)], p0_recv.at[2])
-    low = slots_z[0] + slots_z[1] + slots_z[2] + slots_z[3]
-    high = slots_z[4] + slots_z[5] + slots_z[6] + slots_z[7]
-    rows = jnp.concatenate([low, high], axis=0)
+    await_bytes(slots_p, p0_recv.at[1])
+    coarse = [jnp.sum(slots_p[s], axis=0, keepdims=True) for s in range(8)]
     alpha = None
     cores = []
     for k in range(ITERS):
-        correct(coarse_rows(rows))
+        correct(coarse)
         ri, ii, planes = advance(k, None if k == 0 else jnp.broadcast_to(alpha, (8, LANES)))
         cores.append(share(k, ri, ii, planes))
         wide = None if k == 0 else jnp.broadcast_to(jnp.concatenate([alpha] * TILES, axis=1), (CY, NZ))
         if k < ITERS - 1:
-            halos = smooth(q, k + 1)
+            halos = smooth(q, k + 1, lambda: None)
         update_search(k, wide)
         if k < ITERS - 1:
             operate(k + 1)
             receive_halos(k + 1, halos)
-        rows, alpha = gather(k)
+        coarse, alpha = gather(k)
 
     wide = jnp.broadcast_to(jnp.concatenate([alpha] * TILES, axis=1), (CY, NZ))
 
     def finish(x, carry):
         for f in range(4):
-            sol[f, x] = sol[f, x] + wide * z[f, x]
-            r[f, x] = r[f, x] - wide * q[f, x]
+            sol_h[f, x] = sol[f, x] + wide * z[f, x]
+            res_h[f, x] = r[f, x] - wide * q[f, x]
         return carry
 
     lax.fori_loop(0, CX, finish, 0)
-    outs = [pltpu.make_async_copy(sol, sol_h, out_sem.at[0]), pltpu.make_async_copy(r, res_h, out_sem.at[1])]
+    outs = []
     for copy in outs:
         copy.start()
     for copy in started + cores:
         copy.wait_send()
-    await_bytes(sizes.at[pl.ds(0, 7), :, pl.ds(0, LANES)], p0_send.at[0])
-    await_bytes(sizes.at[pl.ds(0, 3), :, pl.ds(0, LANES)], p0_send.at[1])
-    await_bytes(slots_z.at[pl.ds(0, 7)], p0_send.at[2])
+    await_bytes(sizes.at[pl.ds(0, 7)], p0_send.at[0])
+    await_bytes(sizes.at[pl.ds(0, 62)], p0_send.at[1])
     for k in range(ITERS):
         await_bytes(sizes, all_send.at[k])
     for copy in outs:
@@ -472,21 +468,20 @@
         vmem(3, 4 * KB, 1024), vmem(3, KB, NZ), vmem(14, 8, NZ),
         vmem(2, 2, CY, NZ), vmem(2, 2, CX, NZ), vmem(2, 2, CX, NZ),
         vmem(3, 2, 4, CY, NZ), vmem(3, 2, 4, CX, NZ), vmem(3, 2, 4, CX, NZ),
-        vmem(16, LANES), vmem(8, LANES), vmem(4, LANES), vmem(8, 4, LANES),
-        vmem(3, 1, 2 * LANES), vmem(3, 1, 2 * LANES), vmem(3, 1, 2 * LANES), vmem(3, 128, 2 * LANES),
-        vmem(127, 1, 2 * LANES),
+        vmem(1, LANES), vmem(8, LANES), vmem(2, 1, LANES), vmem(8, 8, LANES),
+        vmem(3, 1, LANES), vmem(3, 1, LANES), vmem(3, 1, LANES), vmem(3, 128, LANES), vmem(127, 1, LANES),
         dma(6), dma(2), dma(8), dma(8), dma(1), dma(3, 2, 4), dma(3), dma(3), dma(3, 2), dma(3), dma(3),
     ]
     hbm = pl.BlockSpec(memory_space=pl.ANY)
-    out = jax.ShapeDtypeStruct((4, *block), F32)
+    out = pltpu.VMEM((4, *block), F32)
     return pl.pallas_call(
         kernel,
         out_shape=(out, out),
         in_specs=[pl.BlockSpec(memory_space=pltpu.SMEM)] + [hbm] * 6,
-        out_specs=(hbm, hbm),
+        out_specs=(pl.BlockSpec(memory_space=pltpu.VMEM),)*2,
         scratch_shapes=scratch,
         compiler_params=pltpu.CompilerParams(
-            collective_id=0, has_side_effects=True, vmem_limit_bytes=48 * 1024 * 1024
+            collective_id=0, has_side_effects=True, vmem_limit_bytes=60 * 1024 * 1024
         ),
     )(extents, source, phase_label, interface, conductivity, admittance, coarse_inverse)
 

time: 65.9 us -> 55.1 us (0.84)
  local copies, waits for them, and re-layouts: 8.7 us -> 1.94 us
  Pallas kernels: 56.2 us -> 52.4 us
    unnamed x16 -> x2, local copies, waits for them, and re-layouts: 8.7 us -> 1.94 us
    pallas_call x1, Pallas kernels: 56.2 us -> 52.4 us  [local(): pl.pallas_call(kernel, out_shape=(out, out), in_specs=[pl.BlockSpec(memor...]
where the time goes in v2:
time: 55.1 us; the launch traced here: 54.9 us
  Pallas kernels  52.4 us (95%)
  local copies, waits for them, and re-layouts  1.94 us (4%)
  between operations  0.64 us (1%)
    pallas_call x1, Pallas kernels, local(): pl.pallas_call(kernel, out_shape=(out, out), in_specs=[pl.BlockSpec(memor...  52.4 us
    unnamed x2, local copies, waits for them, and re-layouts  1.94 us

profile of v2, /device:TPU:1, one launch (start us, length us, event | category | flops | bytes accessed | tf_op | source)
XLA Modules:
  0.0 54.9 jit_solution(17318205862825198700)
XLA Ops:
  0.6 52.4 %shard_map.86 = (f32[4,8,16,512]{3,2,1,0:T(8,128)S(1)}, f32[4,8,16,512]{3,2,1,0:T(8,128)S(1)}) custom-call(s32[1,8]{1,0:T(1,128)} %ext.1, f32[4,8,16,512]{3,2,1,0:T(8,128)} %src_h.1, s32[8,16,512]{2,1,0:T(8,128)} %phase_h.1, s32[8,16,512]{2,1,0:T(8,128)} %inter_h.1, f32[2,8,16,512]{3,2,1,0:T(8,128)} %cond_h.1, f32[2,8,16,512]{3,2,1,0:T(8,128)} %adm_h.1, ...), custom_call_target="tpu_custom_call" | custom-call | tf_op jit(solution)/shard_map/pallas_call | solution.py:477
  53.0 1.0 %copy.11 = f32[4,8,16,512]{3,2,1,0:T(8,128)} copy(f32[4,8,16,512]{3,2,1,0:T(8,128)S(1)} %get-tuple-element.2) | data formatting | bytes 2097152
  54.0 1.0 %copy.12 = f32[4,8,16,512]{3,2,1,0:T(8,128)} copy(f32[4,8,16,512]{3,2,1,0:T(8,128)S(1)} %get-tuple-element.3) | data formatting | bytes 2097152

commit v3 on v2

--- a/solution.py
+++ b/solution.py
@@ -21,10 +21,10 @@
 
 
 def kernel(
-    ext, src_h, phase_h, inter_h, cond_h, adm_h, cinv_h, sol_h, res_h,
+    ext_h, src_h, phase_h, inter_h, cond_h, adm_h, cinv_h, sol_h, res_h,
     r, q, u, z, sol, first, second, cond, phase, inter, adm, cd, cr, sr,
     wx, wym, wyp, wzm, wzp, tw, ee, dinv, wyb, cinv, onehot, table,
-    hxc, hyc, syc, hx, hy, sy, row_z, slots_z, row_p, slots_p, row_c, slots_c, row_all, slots_all, sizes,
+    hxc, hyc, syc, hx, hy, sy, row_z, slots_z, row_p, slots_p, row_c, slots_c, row_all, slots_all, sizes, ext,
     load_sem, out_sem, near_send, near_recv, c_sem, halo_sem, p0_send, p0_recv, core_sem, all_send, all_recv,
 ):
     brick, grp = lax.axis_index("brick"), lax.axis_index("grp")
@@ -48,14 +48,14 @@
 
     loads = [
         load(0, cond_h, cond), load(1, phase_h, phase), load(2, src_h, r),
-        load(3, cinv_h, cinv.at[1]), load(4, inter_h, inter), load(5, adm_h, adm),
+        load(3, cinv_h, cinv.at[1]), load(4, inter_h, inter), load(5, adm_h, adm), load(6, ext_h, ext),
     ]
-    for copy in loads:
-        copy.start()
     barrier = pltpu.get_barrier_semaphore()
     greeted = along_z + plane + [up, down]
     for dev in greeted:
         pl.semaphore_signal(barrier, inc=1, device_id=dev, device_id_type=MESH)
+    for copy in loads:
+        copy.start()
 
     lane = lax.broadcasted_iota(jnp.int32, (8, LANES), 1)
     sub = lax.broadcasted_iota(jnp.int32, (8, LANES), 0)
@@ -71,16 +71,14 @@
     def await_bytes(ref, sem):
         pltpu.make_async_copy(ref, ref, sem).wait()
 
+    loads[6].wait()
     depth = lax.broadcasted_iota(jnp.int32, (KB, NZ), 1)
-    slab = lax.broadcasted_iota(jnp.int32, (KB, NZ), 0)
-    start = jnp.int32(0)
-    begins = jnp.zeros((KB, NZ), jnp.int32)
-    ends = jnp.zeros((KB, NZ), jnp.int32)
-    for k in range(KB):
-        stop = start + ext[0, k]
-        begins = jnp.where(slab == k, start, begins)
-        ends = jnp.where(slab == k, stop, ends)
-        start = stop
+    length = jnp.broadcast_to(ext[...], (KB, KB)).astype(F32)
+    earlier = lax.broadcasted_iota(jnp.int32, (KB, KB), 1) < lax.broadcasted_iota(jnp.int32, (KB, KB), 0)
+    not_later = lax.broadcasted_iota(jnp.int32, (KB, KB), 1) <= lax.broadcasted_iota(jnp.int32, (KB, KB), 0)
+    begins = jnp.sum(jnp.where(earlier, length, 0.0), axis=1, keepdims=True)
+    ends = jnp.sum(jnp.where(not_later, length, 0.0), axis=1, keepdims=True)
+    depth = depth.astype(F32)
     own_onehot = jnp.where((depth >= begins) & (depth < ends), 1.0, 0.0).astype(F32)
     onehot[1] = own_onehot
 
@@ -204,7 +202,7 @@
             + wzm[i, x] * roll(center, 1, 1) + wzp[i, x] * roll(center, -1, 1)
         )
 
-    def smooth(given, k, between):
+    def smoother(given, k):
         out = second.at[k % 2]
 
         def scaled(x, carry):
@@ -223,24 +221,31 @@
                 sy[k, 1, f, pl.ds(x, 1), :] = value[CY - 1 : CY]
             return carry
 
-        lax.fori_loop(0, 4, lambda n, c: scaled(ends(n), c), 0)
-        lax.fori_loop(0, 2, lambda n, c: stencil(n * (CX - 1), c), 0)
         halos = [
             remote(out.at[:, CX], hx.at[k, 0], halo_sem.at[k, 0, 0], halo_sem.at[k, 1, 0], up),
             remote(out.at[:, 1], hx.at[k, 1], halo_sem.at[k, 0, 1], halo_sem.at[k, 1, 1], down),
         ]
-        for copy in halos:
-            copy.start()
-        between()
-        lax.fori_loop(2, CX - 2, scaled, 0)
-        lax.fori_loop(1, CX - 1, stencil, 0)
         sides = [
             remote(sy.at[k, 1], hy.at[k, 0], halo_sem.at[k, 0, 2], halo_sem.at[k, 1, 2], right),
             remote(sy.at[k, 0], hy.at[k, 1], halo_sem.at[k, 0, 3], halo_sem.at[k, 1, 3], left),
         ]
-        for copy in sides:
-            copy.start()
-        return halos + sides
+
+        def edges():
+            lax.fori_loop(0, 4, lambda n, c: scaled(ends(n), c), 0)
+            lax.fori_loop(0, 2, lambda n, c: stencil(n * (CX - 1), c), 0)
+
+        def send():
+            for copy in halos:
+                copy.start()
+
+        def interior():
+            lax.fori_loop(2, CX - 2, scaled, 0)
+            lax.fori_loop(1, CX - 1, stencil, 0)
+            for copy in sides:
+                copy.start()
+            return halos + sides
+
+        return edges, send, interior
 
     def operate(k):
         v = second.at[k % 2]
@@ -329,7 +334,7 @@
                         sums[f] = sums[f] + raised
                 return (ri, ii, *sums)
 
-            ri, ii, *sums = lax.fori_loop(0, CX, step, (ri, ii, zero, zero, zero, zero))
+            ri, ii, *sums = lax.fori_loop(0, CX, step, (ri, ii, zero, zero, zero, zero), unroll=2)
             for f in range(4):
                 planes[f].append(sums[f])
         return ri, ii, [jnp.concatenate(parts, axis=1) for parts in planes]
@@ -353,13 +358,14 @@
     slot = (cz % 4) * 32 + cx * 8 + cy * 2 + cz // 4
     sibling = {"brick": brick, "grp": cx * 2 + 1 - core}
 
-    def share(k, ri, ii, planes):
-        coarse = restrict_row(planes, 0)
+    def share(k, ri, ii, planes, edges, send_halos):
+        coarse = restrict_row(planes, 0) if k < ITERS - 1 else jnp.zeros((1, LANES), F32)
         ri = jnp.sum(jnp.sum(ri, axis=0, keepdims=True), axis=1, keepdims=True)
         ii = jnp.sum(jnp.sum(ii, axis=0, keepdims=True), axis=1, keepdims=True)
         row_c[k] = jnp.where(lane[0:1] < 32, coarse, jnp.where(lane[0:1] < 64, ri, ii))
         copy = remote(row_c.at[k], slots_c.at[k], core_sem.at[k, 0], core_sem.at[k, 1], sibling)
         copy.start()
+        edges()
         copy.wait_recv()
         row_all[k] = row_c[k] + slots_c[k]
 
@@ -383,6 +389,7 @@
         pltpu.make_async_copy(
             row_all.at[k], slots_all.at[k, pl.ds(slot, 1)], all_recv.at[k]
         ).start()
+        send_halos()
         return copy
 
     def gather(k):
@@ -409,7 +416,11 @@
         pltpu.make_async_copy(row_p, mine, p0_recv.at[1]).start()
         lax.fori_loop(2, CX - 2, weigh, 0)
 
-    halos = smooth(r, 0, pass_on)
+    edges, send_halos, interior = smoother(r, 0)
+    edges()
+    send_halos()
+    pass_on()
+    halos = interior()
     operate(0)
     receive_halos(0, halos)
     for copy in (hot_up, hot_down, cinv_up, cinv_down):
@@ -421,10 +432,11 @@
     for k in range(ITERS):
         correct(coarse)
         ri, ii, planes = advance(k, None if k == 0 else jnp.broadcast_to(alpha, (8, LANES)))
-        cores.append(share(k, ri, ii, planes))
+        edges, send_halos, interior = smoother(q, k + 1) if k < ITERS - 1 else (lambda: None,) * 3
+        cores.append(share(k, ri, ii, planes, edges, send_halos))
         wide = None if k == 0 else jnp.broadcast_to(jnp.concatenate([alpha] * TILES, axis=1), (CY, NZ))
         if k < ITERS - 1:
-            halos = smooth(q, k + 1, lambda: None)
+            halos = interior()
         update_search(k, wide)
         if k < ITERS - 1:
             operate(k + 1)
@@ -470,14 +482,15 @@
         vmem(3, 2, 4, CY, NZ), vmem(3, 2, 4, CX, NZ), vmem(3, 2, 4, CX, NZ),
         vmem(1, LANES), vmem(8, LANES), vmem(2, 1, LANES), vmem(8, 8, LANES),
         vmem(3, 1, LANES), vmem(3, 1, LANES), vmem(3, 1, LANES), vmem(3, 128, LANES), vmem(127, 1, LANES),
-        dma(6), dma(2), dma(8), dma(8), dma(1), dma(3, 2, 4), dma(3), dma(3), dma(3, 2), dma(3), dma(3),
+        pltpu.VMEM((1, KB), jnp.int32),
+        dma(7), dma(2), dma(8), dma(8), dma(1), dma(3, 2, 4), dma(3), dma(3), dma(3, 2), dma(3), dma(3),
     ]
     hbm = pl.BlockSpec(memory_space=pl.ANY)
     out = pltpu.VMEM((4, *block), F32)
     return pl.pallas_call(
         kernel,
         out_shape=(out, out),
-        in_specs=[pl.BlockSpec(memory_space=pltpu.SMEM)] + [hbm] * 6,
+        in_specs=[hbm] * 7,
         out_specs=(pl.BlockSpec(memory_space=pltpu.VMEM),)*2,
         scratch_shapes=scratch,
         compiler_params=pltpu.CompilerParams(

time: 55.1 us -> 53.6 us (0.973)
  Pallas kernels: 52.4 us -> 50.9 us
    pallas_call x1, Pallas kernels: 52.4 us -> 50.9 us  [local(): pl.pallas_call(kernel, out_shape=(out, out), in_specs=[hbm] * 7, out_spec...]
where the time goes in v3:
time: 53.6 us; the launch traced here: 53.5 us
  Pallas kernels  50.9 us (95%)
  local copies, waits for them, and re-layouts  1.94 us (4%)
  between operations  0.64 us (1%)
    pallas_call x1, Pallas kernels, local(): pl.pallas_call(kernel, out_shape=(out, out), in_specs=[hbm] * 7, out_spec...  50.9 us
    unnamed x2, local copies, waits for them, and re-layouts  1.94 us

profile of v3, /device:TPU:1, one launch (start us, length us, event | category | flops | bytes accessed | tf_op | source)
XLA Modules:
  0.0 53.5 jit_solution(9605285366941983181)
XLA Ops:
  0.6 50.9 %shard_map.86 = (f32[4,8,16,512]{3,2,1,0:T(8,128)S(1)}, f32[4,8,16,512]{3,2,1,0:T(8,128)S(1)}) custom-call(s32[1,8]{1,0:T(1,128)} %ext_h.1, f32[4,8,16,512]{3,2,1,0:T(8,128)} %src_h.1, s32[8,16,512]{2,1,0:T(8,128)} %phase_h.1, s32[8,16,512]{2,1,0:T(8,128)} %inter_h.1, f32[2,8,16,512]{3,2,1,0:T(8,128)} %cond_h.1, f32[2,8,16,512]{3,2,1,0:T(8,128)} %adm_h.1, ...), custom_call_target="tpu_custom_call" | custom-call | tf_op jit(solution)/shard_map/pallas_call | solution.py:490
  51.5 1.0 %copy.11 = f32[4,8,16,512]{3,2,1,0:T(8,128)} copy(f32[4,8,16,512]{3,2,1,0:T(8,128)S(1)} %get-tuple-element.2) | data formatting | bytes 2097152
  52.5 1.0 %copy.12 = f32[4,8,16,512]{3,2,1,0:T(8,128)} copy(f32[4,8,16,512]{3,2,1,0:T(8,128)S(1)} %get-tuple-element.3) | data formatting | bytes 2097152

commit v4 on v3

--- a/solution.py
+++ b/solution.py
@@ -24,7 +24,7 @@
     ext_h, src_h, phase_h, inter_h, cond_h, adm_h, cinv_h, sol_h, res_h,
     r, q, u, z, sol, first, second, cond, phase, inter, adm, cd, cr, sr,
     wx, wym, wyp, wzm, wzp, tw, ee, dinv, wyb, cinv, onehot, table,
-    hxc, hyc, syc, hx, hy, sy, row_z, slots_z, row_p, slots_p, row_c, slots_c, row_all, slots_all, sizes, ext,
+    hxc, hyc, syc, hx, hy, sy, row_z, slots_z, row_p, slots_p, row_c, slots_c, row_all, slots_all, sizes, ext, total,
     load_sem, out_sem, near_send, near_recv, c_sem, halo_sem, p0_send, p0_recv, core_sem, all_send, all_recv,
 ):
     brick, grp = lax.axis_index("brick"), lax.axis_index("grp")
@@ -263,11 +263,8 @@
         lax.fori_loop(0, CX, stencil, 0)
 
     def receive_halos(k, copies):
-        for copy in copies:
+        for copy in copies[2:]:
             copy.wait_recv()
-        for f in range(4):
-            u[f, 0] = u[f, 0] - wx[f // 2, 0] * hx[k, 0, f]
-            u[f, CX - 1] = u[f, CX - 1] - wx[f // 2, CX] * hx[k, 1, f]
 
         def rows(x, carry):
             for f in range(4):
@@ -278,6 +275,11 @@
             return carry
 
         lax.fori_loop(0, CX, rows, 0)
+        for copy in copies[:2]:
+            copy.wait_recv()
+        for f in range(4):
+            u[f, 0] = u[f, 0] - wx[f // 2, 0] * hx[k, 0, f]
+            u[f, CX - 1] = u[f, CX - 1] - wx[f // 2, CX] * hx[k, 1, f]
         for copy in copies:
             copy.wait_send()
 
@@ -303,10 +305,9 @@
 
     def advance(k, alpha):
         zero = jnp.zeros((8, LANES), F32)
-        ri, ii = zero, zero
-        planes = [[] for _ in range(4)]
-        for t in range(TILES):
-            lanes = slice(LANES * t, LANES * (t + 1))
+
+        def tile(t, dots):
+            lanes = pl.ds(pl.multiple_of(LANES * t, LANES), LANES)
             p = [table[n, :, lanes] for n in range(14)]
 
             def step(x, carry):
@@ -334,10 +335,13 @@
                         sums[f] = sums[f] + raised
                 return (ri, ii, *sums)
 
-            ri, ii, *sums = lax.fori_loop(0, CX, step, (ri, ii, zero, zero, zero, zero), unroll=2)
-            for f in range(4):
-                planes[f].append(sums[f])
-        return ri, ii, [jnp.concatenate(parts, axis=1) for parts in planes]
+            ri, ii, *sums = lax.fori_loop(0, CX, step, (*dots, zero, zero, zero, zero), unroll=4)
+            for f in range(4):
+                total[f, :, lanes] = sums[f]
+            return ri, ii
+
+        ri, ii = lax.fori_loop(0, TILES, tile, (zero, zero))
+        return ri, ii, total
 
     def update_search(k, alpha):
         smoothed = second.at[k % 2]
@@ -482,7 +486,7 @@
         vmem(3, 2, 4, CY, NZ), vmem(3, 2, 4, CX, NZ), vmem(3, 2, 4, CX, NZ),
         vmem(1, LANES), vmem(8, LANES), vmem(2, 1, LANES), vmem(8, 8, LANES),
         vmem(3, 1, LANES), vmem(3, 1, LANES), vmem(3, 1, LANES), vmem(3, 128, LANES), vmem(127, 1, LANES),
-        pltpu.VMEM((1, KB), jnp.int32),
+        pltpu.VMEM((1, KB), jnp.int32), vmem(4, 8, NZ),
         dma(7), dma(2), dma(8), dma(8), dma(1), dma(3, 2, 4), dma(3), dma(3), dma(3, 2), dma(3), dma(3),
     ]
     hbm = pl.BlockSpec(memory_space=pl.ANY)

time: 53.6 us -> 53.2 us (level)
  no operation moved by 1% of the time
where the time goes in v4:
time: 53.2 us; the launch traced here: 53.1 us
  Pallas kernels  50.5 us (95%)
  local copies, waits for them, and re-layouts  1.94 us (4%)
  between operations  0.64 us (1%)
    pallas_call x1, Pallas kernels, local(): pl.pallas_call(kernel, out_shape=(out, out), in_specs=[hbm] * 7, out_spec...  50.5 us
    unnamed x2, local copies, waits for them, and re-layouts  1.94 us

profile of v4, /device:TPU:1, one launch (start us, length us, event | category | flops | bytes accessed | tf_op | source)
XLA Modules:
  0.0 53.1 jit_solution(14173263858918400348)
XLA Ops:
  0.6 50.5 %shard_map.86 = (f32[4,8,16,512]{3,2,1,0:T(8,128)S(1)}, f32[4,8,16,512]{3,2,1,0:T(8,128)S(1)}) custom-call(s32[1,8]{1,0:T(1,128)} %ext_h.1, f32[4,8,16,512]{3,2,1,0:T(8,128)} %src_h.1, s32[8,16,512]{2,1,0:T(8,128)} %phase_h.1, s32[8,16,512]{2,1,0:T(8,128)} %inter_h.1, f32[2,8,16,512]{3,2,1,0:T(8,128)} %cond_h.1, f32[2,8,16,512]{3,2,1,0:T(8,128)} %adm_h.1, ...), custom_call_target="tpu_custom_call" | custom-call | tf_op jit(solution)/shard_map/pallas_call | solution.py:494
  51.1 1.0 %copy.11 = f32[4,8,16,512]{3,2,1,0:T(8,128)} copy(f32[4,8,16,512]{3,2,1,0:T(8,128)S(1)} %get-tuple-element.2) | data formatting | bytes 2097152
  52.1 1.0 %copy.12 = f32[4,8,16,512]{3,2,1,0:T(8,128)} copy(f32[4,8,16,512]{3,2,1,0:T(8,128)S(1)} %get-tuple-element.3) | data formatting | bytes 2097152

commit v5 on v4

--- a/solution.py
+++ b/solution.py
@@ -277,13 +277,10 @@
         lax.fori_loop(0, CX, rows, 0)
         for copy in copies[:2]:
             copy.wait_recv()
-        for f in range(4):
-            u[f, 0] = u[f, 0] - wx[f // 2, 0] * hx[k, 0, f]
-            u[f, CX - 1] = u[f, CX - 1] - wx[f // 2, CX] * hx[k, 1, f]
         for copy in copies:
             copy.wait_send()
 
-    def correct(coarse):
+    def correct(k, coarse):
         profile = []
         for j in range(3):
             per_field = []
@@ -300,8 +297,8 @@
         for n, value in enumerate(rows):
             table[n] = jnp.broadcast_to(value, (8, NZ))
         for f in range(4):
-            u[f, 0] = u[f, 0] - wx[f // 2, 0] * (profile[0][f] - own[f])
-            u[f, CX - 1] = u[f, CX - 1] - wx[f // 2, CX] * (profile[2][f] - own[f])
+            u[f, 0] = u[f, 0] - wx[f // 2, 0] * (hx[k, 0, f] + (profile[0][f] - own[f]))
+            u[f, CX - 1] = u[f, CX - 1] - wx[f // 2, CX] * (hx[k, 1, f] + (profile[2][f] - own[f]))
 
     def advance(k, alpha):
         zero = jnp.zeros((8, LANES), F32)
@@ -434,7 +431,7 @@
     alpha = None
     cores = []
     for k in range(ITERS):
-        correct(coarse)
+        correct(k, coarse)
         ri, ii, planes = advance(k, None if k == 0 else jnp.broadcast_to(alpha, (8, LANES)))
         edges, send_halos, interior = smoother(q, k + 1) if k < ITERS - 1 else (lambda: None,) * 3
         cores.append(share(k, ri, ii, planes, edges, send_halos))

time: 53.2 us -> 53.1 us (level)
  no operation moved by 1% of the time
where the time goes in v5:
time: 53.1 us; the launch traced here: 53 us
  Pallas kernels  50.4 us (95%)
  local copies, waits for them, and re-layouts  1.94 us (4%)
  between operations  0.64 us (1%)
    pallas_call x1, Pallas kernels, local(): pl.pallas_call(kernel, out_shape=(out, out), in_specs=[hbm] * 7, out_spec...  50.4 us
    unnamed x2, local copies, waits for them, and re-layouts  1.94 us

profile of v5, /device:TPU:1, one launch (start us, length us, event | category | flops | bytes accessed | tf_op | source)
XLA Modules:
  0.0 53.0 jit_solution(9188184841735398853)
XLA Ops:
  0.6 50.4 %shard_map.86 = (f32[4,8,16,512]{3,2,1,0:T(8,128)S(1)}, f32[4,8,16,512]{3,2,1,0:T(8,128)S(1)}) custom-call(s32[1,8]{1,0:T(1,128)} %ext_h.1, f32[4,8,16,512]{3,2,1,0:T(8,128)} %src_h.1, s32[8,16,512]{2,1,0:T(8,128)} %phase_h.1, s32[8,16,512]{2,1,0:T(8,128)} %inter_h.1, f32[2,8,16,512]{3,2,1,0:T(8,128)} %cond_h.1, f32[2,8,16,512]{3,2,1,0:T(8,128)} %adm_h.1, ...), custom_call_target="tpu_custom_call" | custom-call | tf_op jit(solution)/shard_map/pallas_call | solution.py:491
  51.0 1.0 %copy.11 = f32[4,8,16,512]{3,2,1,0:T(8,128)} copy(f32[4,8,16,512]{3,2,1,0:T(8,128)S(1)} %get-tuple-element.2) | data formatting | bytes 2097152
  52.0 1.0 %copy.12 = f32[4,8,16,512]{3,2,1,0:T(8,128)} copy(f32[4,8,16,512]{3,2,1,0:T(8,128)S(1)} %get-tuple-element.3) | data formatting | bytes 2097152

commit v6 on v5

--- a/solution.py
+++ b/solution.py
@@ -21,11 +21,11 @@
 
 
 def kernel(
-    ext_h, src_h, phase_h, inter_h, cond_h, adm_h, cinv_h, sol_h, res_h,
-    r, q, u, z, sol, first, second, cond, phase, inter, adm, cd, cr, sr,
+    ext_h, src_h, phase_h, inter_h, cond_h, adm_h, cinv_h, sol, z, r, q, last_alpha,
+    u, first, second, cond, phase, inter, adm, cd, cr, sr,
     wx, wym, wyp, wzm, wzp, tw, ee, dinv, wyb, cinv, onehot, table,
     hxc, hyc, syc, hx, hy, sy, row_z, slots_z, row_p, slots_p, row_c, slots_c, row_all, slots_all, sizes, ext, total,
-    load_sem, out_sem, near_send, near_recv, c_sem, halo_sem, p0_send, p0_recv, core_sem, all_send, all_recv,
+    load_sem, near_send, near_recv, c_sem, halo_sem, p0_send, p0_recv, core_sem, all_send, all_recv,
 ):
     brick, grp = lax.axis_index("brick"), lax.axis_index("grp")
     cy, cz, cx, core = brick // 8, brick % 8, grp // 2, grp % 2
@@ -444,26 +444,13 @@
             receive_halos(k + 1, halos)
         coarse, alpha = gather(k)
 
-    wide = jnp.broadcast_to(jnp.concatenate([alpha] * TILES, axis=1), (CY, NZ))
-
-    def finish(x, carry):
-        for f in range(4):
-            sol_h[f, x] = sol[f, x] + wide * z[f, x]
-            res_h[f, x] = r[f, x] - wide * q[f, x]
-        return carry
-
-    lax.fori_loop(0, CX, finish, 0)
-    outs = []
-    for copy in outs:
-        copy.start()
+    last_alpha[0, 0] = jnp.broadcast_to(jnp.concatenate([alpha] * TILES, axis=1), (CY, NZ))
     for copy in started + cores:
         copy.wait_send()
     await_bytes(sizes.at[pl.ds(0, 7)], p0_send.at[0])
     await_bytes(sizes.at[pl.ds(0, 62)], p0_send.at[1])
     for k in range(ITERS):
         await_bytes(sizes, all_send.at[k])
-    for copy in outs:
-        copy.wait()
 
 
 def local(source, phase_label, interface, conductivity, admittance, extents, coarse_inverse):
@@ -473,7 +460,7 @@
     ints = pltpu.VMEM(block, jnp.int32)
     dma = lambda *shape: pltpu.SemaphoreType.DMA(shape)
     scratch = [
-        vmem(4, *block), vmem(4, *block), vmem(4, *block), vmem(4, *block), vmem(4, *block),
+        vmem(4, *block),
         vmem(4, *padded), vmem(2, 4, *padded), vmem(2, *block), ints, ints, vmem(2, *block),
         vmem(2, *padded), vmem(*block), vmem(*block),
         vmem(2, CX + 1, CY, NZ), vmem(2, *block), vmem(2, *block), vmem(2, *block), vmem(2, *block),
@@ -484,20 +471,22 @@
         vmem(1, LANES), vmem(8, LANES), vmem(2, 1, LANES), vmem(8, 8, LANES),
         vmem(3, 1, LANES), vmem(3, 1, LANES), vmem(3, 1, LANES), vmem(3, 128, LANES), vmem(127, 1, LANES),
         pltpu.VMEM((1, KB), jnp.int32), vmem(4, 8, NZ),
-        dma(7), dma(2), dma(8), dma(8), dma(1), dma(3, 2, 4), dma(3), dma(3), dma(3, 2), dma(3), dma(3),
+        dma(7), dma(8), dma(8), dma(1), dma(3, 2, 4), dma(3), dma(3), dma(3, 2), dma(3), dma(3),
     ]
     hbm = pl.BlockSpec(memory_space=pl.ANY)
     out = pltpu.VMEM((4, *block), F32)
-    return pl.pallas_call(
+    in_vmem = pl.BlockSpec(memory_space=pltpu.VMEM)
+    iterate, search, residual, image, alpha = pl.pallas_call(
         kernel,
-        out_shape=(out, out),
+        out_shape=(out, out, out, out, pltpu.VMEM((1, 1, CY, NZ), F32)),
         in_specs=[hbm] * 7,
-        out_specs=(pl.BlockSpec(memory_space=pltpu.VMEM),)*2,
+        out_specs=(in_vmem,) * 5,
         scratch_shapes=scratch,
         compiler_params=pltpu.CompilerParams(
-            collective_id=0, has_side_effects=True, vmem_limit_bytes=60 * 1024 * 1024
+            collective_id=0, has_side_effects=True, vmem_limit_bytes=59 * 1024 * 1024
         ),
     )(extents, source, phase_label, interface, conductivity, admittance, coarse_inverse)
+    return iterate + alpha * search, residual - alpha * image
 
 
 def solution(mesh):

time: 53.1 us -> 52.9 us (level)
  other arithmetic: 0 us -> 2.02 us
  local copies, waits for them, and re-layouts: 1.94 us -> 0 us
    sub x0 -> x1, other arithmetic: none -> 2.02 us  [local(): return (iterate + alpha * search, residual - alpha * image)]
    unnamed x2 -> x0, local copies, waits for them, and re-layouts: 1.94 us -> none
where the time goes in v6:
time: 52.9 us; the launch traced here: 52.8 us
  Pallas kernels  50.2 us (95%)
  other arithmetic  2.02 us (4%)
  between operations  0.64 us (1%)
    pallas_call x1, Pallas kernels, local(): pl.pallas_call(kernel, out_shape=(out, out, out, out, pltpu.VMEM((1, 1, C...  50.2 us
    sub x1, other arithmetic, local(): return (iterate + alpha * search, residual - alpha * image)  2.02 us

profile of v6, /device:TPU:1, one launch (start us, length us, event | category | flops | bytes accessed | tf_op | source)
XLA Modules:
  0.0 52.8 jit_solution(14050355897387775369)
XLA Ops:
  0.6 50.2 %shard_map.86 = (f32[4,8,16,512]{3,2,1,0:T(8,128)S(1)}, f32[4,8,16,512]{3,2,1,0:T(8,128)S(1)}, f32[4,8,16,512]{3,2,1,0:T(8,128)S(1)}, f32[4,8,16,512]{3,2,1,0:T(8,128)S(1)}, f32[1,1,16,512]{3,2,1,0:T(8,128)S(1)}) custom-call(s32[1,8]{1,0:T(1,128)} %ext_h.1, f32[4,8,16,512]{3,2,1,0:T(8,128)} %src_h.1, s32[8,16,512]{2,1,0:T(8,128)} %phase_h.1, ...), custom_call_target="tpu_custom_call" | custom-call | tf_op jit(solution)/shard_map/pallas_call | solution.py:479
  50.8 2.0 %multiply_subtract_fusion = (f32[4,8,16,512]{3,2,1,0:T(8,128)}, f32[4,8,16,512]{3,2,1,0:T(8,128)}) fusion(f32[4,8,16,512]{3,2,1,0:T(8,128)S(1)} %get-tuple-element.10, f32[4,8,16,512]{3,2,1,0:T(8,128)S(1)} %get-tuple-element.11, f32[16,512]{1,0:T(8,128)S(1)} %bitcast.1, f32[4,8,16,512]{3,2,1,0:T(8,128)S(1)} %get-tuple-element.7, ...), kind=kLoop, calls=%fused_computation | loop fusion | flops 1048576 | bytes 6324224 | tf_op jit(solution)/shard_map/sub | solution.py:489
